TPU v7x, 256 devices: a whole 4x4x8 slice. The times are simulated.
256 devices in a mesh: band: 32 (over x_hi, z, core), fft: 8 (over y, x_lo).
Axes of the slice: x: 4 (x_hi: 2, x_lo: 2; x = x_hi * 2 + x_lo), y: 4, z: 8, core: 2. Of those that a mesh axis runs over, the one named last changes fastest.
Arguments:
- coefficients: float32 [32, 675840], P(None, ('band', 'fft')), may hold values from -0.01171875 to 0.01171875
- owned_sticks: int32 [8, 704], P('fft'), may hold values from -1 to 351, as said below
- stick_counts: int32 [8, 352], P('fft'), may hold values from 61 to 119, as said below
- stick_columns: int32 [8, 352], P('fft'), may hold values from 0 to 1799, as said below
- band_order: int32 [32], replicated, may hold values from 0 to 31, each once
Outputs:
- exchange_field: float32 [32, 120, 14400], P('band', 'fft')
Inputs may be any that keep to these rules, and one draw needn't show every extreme that they name: `owned_sticks`: in each row every stick number appears exactly once; each block of 22 entries lists the sticks of one owner along band, -1 marking an empty slot; in each row one owner fills all 22 slots. `stick_counts`: Odd; each row has a stick with 120 - 1 G-vectors. `stick_columns`: the sticks of one row lie in distinct columns. `band_order`: each band appears once.
All inputs are finite; a program needn't handle non-finite values.
Results may differ from a plain program's by a relative error of at most 0.0003.
Values sent between devices are 32-bit elements; how exact they have to be, the bound alone decides.
A program may use at most 128 MiB of HBM per device.

v0:
```python
import math

import jax
import jax.numpy as jnp
from jax import lax
from jax.sharding import PartitionSpec as P

NX = 120
NY = 120
NZ = 120
STOPS = 1


COULOMB = 0.25
EXCHANGE_FRACTION = 0.25
PRECISE = lax.Precision.HIGHEST


def from_behind(x, axis, by):
    count = lax.axis_size(axis)
    return lax.ppermute(x, axis, [(i, (i + by) % count) for i in range(count)])


def centered(position, length):
    return jnp.where(position > length // 2, position - length, position)


def cas_table(length):
    index_row = jnp.arange(length, dtype=jnp.int32)
    phase_step = index_row[:, None] * index_row[None, :] % length
    angle_rad = phase_step.astype(jnp.float32) * (2.0 * math.pi / length)
    return jnp.cos(angle_rad) + jnp.sin(angle_rad)


def planar(field_in, hart_x, hart_y):
    item_count, plane_count, flat_size = field_in.shape
    cube_view = field_in.reshape(item_count, plane_count, NX, NY)
    cube_view = jnp.einsum("pzxy,yl->pzxl", cube_view, hart_y, precision=PRECISE)
    cube_view = jnp.einsum("pzxl,xk->pzkl", cube_view, hart_x, precision=PRECISE)
    return cube_view.reshape(item_count, plane_count, flat_size)


def potential(density, hart_x, hart_y, hart_z, kernel):
    spectrum = planar(density, hart_x, hart_y)
    along_z = (
        jnp.einsum(
            "pzc,zk->pkc",
            lax.all_to_all(spectrum, "fft", split_axis=2, concat_axis=1, tiled=True),
            hart_z,
            precision=PRECISE,
        )
        * kernel[None]
    )
    back_z = jnp.einsum("pkc,kz->pzc", along_z, hart_z, precision=PRECISE)
    mapped = lax.all_to_all(back_z, "fft", split_axis=1, concat_axis=2, tiled=True)
    return planar(mapped, hart_x, hart_y)


def pair_potentials(left_set, right_set, tables):
    left_count = left_set.shape[0]
    right_count = right_set.shape[0]
    density = (left_set[:, None] * right_set[None, :]).reshape(
        left_count * right_count, left_set.shape[1], left_set.shape[2]
    )
    solved = potential(density, tables[0], tables[1], tables[2], tables[3])
    return solved.reshape(left_count, right_count, left_set.shape[1], left_set.shape[2])


def local(coefficients, owned_sticks, stick_counts, stick_columns, band_order):
    band_total = band_order.shape[0]
    groups = lax.axis_size("band")
    fft_count = lax.axis_size("fft")
    per_group = band_total // groups
    own_cap = owned_sticks.shape[1] // groups
    slot_total = stick_counts.shape[1]
    columns = NX * NY // fft_count
    band_index = lax.axis_index("band")
    fft_index = lax.axis_index("fft")
    z_freq = centered(jnp.arange(NZ, dtype=jnp.int32), NZ)
    slot_ids = jnp.arange(slot_total, dtype=jnp.int32)
    my_list = lax.dynamic_slice_in_dim(owned_sticks[0], band_index * own_cap, own_cap)
    matches = my_list[:, None] == slot_ids[None, :]
    my_counts = jnp.sum(jnp.where(matches, stick_counts[0][None, :], 0), axis=1)
    keep_mask = jnp.abs(z_freq)[None, :] <= ((my_counts - 1) // 2)[:, None]
    row_data = coefficients.reshape(band_total, own_cap, NZ)[band_order]
    row_data = jnp.where(keep_mask[None], row_data, 0.0).reshape(groups, per_group, own_cap * NZ)
    arrived = lax.all_to_all(row_data, "band", split_axis=0, concat_axis=2, tiled=True)
    arrived = arrived.reshape(per_group, groups * own_cap, NZ)
    hart_x = cas_table(NX)
    hart_y = cas_table(NY)
    hart_z = cas_table(NZ)
    along_z = jnp.einsum("brk,kz->bzr", arrived, hart_z, precision=PRECISE)
    all_ids = owned_sticks[0]
    hits_table = all_ids[:, None] == slot_ids[None, :]
    place_at = jnp.sum(jnp.where(hits_table, stick_columns[0][None, :], 0), axis=1)
    place_at = jnp.where(all_ids >= 0, place_at, columns)
    col_grid = (
        jnp.zeros((per_group, NZ, columns), jnp.float32)
        .at[:, :, place_at]
        .set(along_z, mode="drop")
    )
    planes = lax.all_to_all(col_grid, "fft", split_axis=1, concat_axis=2, tiled=True)
    orbital = planar(planes, hart_x, hart_y)
    col_glob = fft_index * columns + jnp.arange(columns, dtype=jnp.int32)
    x_freq = centered(col_glob // NY, NX)
    y_freq = centered(col_glob % NY, NY)
    squares = (z_freq * z_freq)[:, None] + (x_freq * x_freq + y_freq * y_freq)[None, :]
    volume = NX * NY * NZ
    scale_factor = COULOMB * math.sqrt(volume) / volume
    kernel = jnp.where(
        squares > 0, scale_factor / jnp.maximum(squares.astype(jnp.float32), 1.0), 0.0
    )
    tables = (hart_x, hart_y, hart_z, kernel)
    own_part = pair_potentials(orbital, orbital, tables)
    exchange_sum = jnp.sum(own_part * orbital[None], axis=1)
    carried = jnp.stack([orbital, jnp.zeros_like(orbital)])
    carried = from_behind(carried, "band", 1)
    linked = pair_potentials(orbital, carried[0], tables)
    exchange_sum = exchange_sum + jnp.sum(linked * carried[0][None], axis=1)
    gained = carried[1] + jnp.sum(linked * orbital[:, None], axis=0)
    carried = jnp.stack([carried[0], gained])
    exchange_sum = exchange_sum + from_behind(carried[1], "band", -STOPS)
    return -EXCHANGE_FRACTION * exchange_sum


def solution(mesh):
    placed = (P(None, ("band", "fft")), P("fft", None), P("fft", None), P("fft", None), P())
    return jax.shard_map(
        local, mesh=mesh, in_specs=placed, out_specs=P("band", "fft", None), check_vma=False
    )
```

profile of v0, /device:TPU:2, one launch (start us, length us, event | category | flops | bytes accessed | tf_op | source)
XLA Modules:
  0.0 375.2 jit_solution(7099931978018082585)
XLA Ops:
  0.0 0.7 compare_select_fusion.3
  0.7 0.7 reduce.3
  1.4 0.8 dynamic-slice_bitcast_fusion
  2.6 1.2 reshape.310
  3.9 0.6 gather_fusion
  4.7 1.1 copy.55
  5.8 10.4 %all-to-all-start = ((f32[32,1,2640]{2,1,0:T(1,128)}), f32[32,1,2640]{2,1,0:T(1,128)S(1)}, u32[]{:S(2)}, u32[]{:S(2)}) async-start(f32[32,1,2640]{2,1,0:T(1,128)} %copy.55), calls=%async_computation | async-start | bytes 688128 | tf_op jit(solution)/shard_map/all_to_all | solution.py:87
  16.6 16.0 %all-to-all-done = f32[32,1,2640]{2,1,0:T(1,128)S(1)} async-done(((f32[32,1,2640]{2,1,0:T(1,128)}), f32[32,1,2640]{2,1,0:T(1,128)S(1)}, u32[]{:S(2)}, u32[]{:S(2)}) %all-to-all-start) | async-done | bytes 337952 | tf_op jit(solution)/shard_map/all_to_all | solution.py:87
  32.6 0.8 reduce.5
  33.7 0.7 fusion.31
  34.4 4.4 %scatter_custom_fusion = f32[120,1800]{0,1:T(8,128)S(1)} fusion(s32[704]{0:T(1024)S(1)} %fusion.40, f32[704,120]{1,0:T(8,128)S(1)} %fusion.31, f32[]{:T(128)} %constant.74.clone.1), kind=kCustom, calls=%fused_computation.28 | custom fusion | bytes 864004 | tf_op jit(solution)/shard_map/scatter | solution.py:100
  38.7 0.9 copy.57
  39.7 18.0 %all_to_all.84 = f32[1,120,1800]{2,0,1:T(1,128)S(1)} all-to-all(f32[1,120,1800]{2,0,1:T(1,128)S(1)} %copy.57), channel_id=1, replica_groups=mesh['band'=32,'fft'=8] {'fft'}, dimensions={1} | all-to-all | bytes 1728000 | tf_op jit(solution)/shard_map/all_to_all | solution.py:102
  57.8 0.9 reshape.312
  58.6 1.9 fusion.21
  60.5 1.2 convolution_bitcast_fusion.6
  61.7 1.6 broadcast_in_dim_reshape.2
  63.3 0.6 stack.3
  63.9 0.6 collective-permute-start
  64.5 25.2 %collective-permute-done = f32[2,1,15,14400]{3,0,2,1:T(2,128)S(1)} collective-permute-done((f32[2,1,15,14400]{3,0,2,1:T(2,128)S(1)}, f32[2,1,15,14400]{3,0,2,1:T(2,128)S(1)}, u32[]{:S(2)}, u32[]{:S(2)}) %collective-permute-start) | collective-permute-done | bytes 1728032 | tf_op jit(solution)/shard_map/ppermute | solution.py:21
  89.7 1.2 copy-done
  90.9 4.4 %multiply_reduce_fusion = f32[15,14400]{1,0:T(8,128)S(1)} fusion(f32[1,1,15,14400]{3,0,2,1:T(1,128)S(1)} %broadcast_in_dim_reshape.2, f32[2,1,15,14400]{3,0,2,1:T(2,128)S(1)} %collective-permute-done), kind=kLoop, calls=%fused_computation.27 | loop fusion | flops 216000 | bytes 2592000 | tf_op jit(solution)/shard_map/mul | solution.py:62
  95.3 1.6 reshape.317
  96.9 3.0 fusion.16
  100.0 1.2 convolution_bitcast_fusion.3
  101.2 4.6 %copy.85 = f32[1,15,120,120]{1,3,2,0:T(8,128)} copy(f32[1,15,120,120]{3,2,1,0:T(8,128)S(1)} %convolution_bitcast_fusion.3) | data formatting | bytes 1728000 | tf_op jit(solution)/shard_map/reshape | solution.py:40
  105.8 0.6 broadcast.280
  106.4 65.8 %reduce.10 = f32[14400,15]{1,0:T(8,128)} reduce(f32[14400,1,15]{2,1,0:T(1,128)} %bitcast.122, f32[]{:T(128)} %broadcast.280), dimensions={1}, to_apply=%bitcast.101.reduce_sub_computation | reduce | bytes 1728004
  172.2 8.0 %reshape.356 = f32[8,1,27000]{2,1,0:T(1,128)} reshape(f32[14400,15]{1,0:T(8,128)} %reduce.10) | data formatting | bytes 1728000
  180.2 4.9 %all-to-all-start.4 = ((f32[8,1,27000]{2,1,0:T(1,128)}), f32[8,1,27000]{2,1,0:T(1,128)S(1)}, u32[]{:S(2)}, u32[]{:S(2)}) async-start(f32[8,1,27000]{2,1,0:T(1,128)} %reshape.356), calls=%async_computation.4 | async-start | bytes 1728512 | tf_op jit(solution)/shard_map/all_to_all | solution.py:48
  185.1 1.9 fusion.4
  187.0 1.2 convolution_bitcast_fusion.5
  188.2 4.5 %copy.81 = f32[1,15,120,120]{1,3,2,0:T(8,128)} copy(f32[1,15,120,120]{3,2,1,0:T(8,128)S(1)} %convolution_bitcast_fusion.5) | data formatting | bytes 1728000 | tf_op jit(solution)/shard_map/reshape | solution.py:40
  192.7 65.8 %reduce.12 = f32[14400,15]{1,0:T(8,128)} reduce(f32[14400,1,15]{2,1,0:T(1,128)} %bitcast.123, f32[]{:T(128)} %broadcast.280), dimensions={1}, to_apply=%bitcast.103.reduce_sub_computation | reduce | bytes 1728004
  258.5 7.9 %reshape.358 = f32[8,1,27000]{2,1,0:T(1,128)} reshape(f32[14400,15]{1,0:T(8,128)} %reduce.12) | data formatting | bytes 1728000
  266.5 6.2 %all-to-all-start.2 = ((f32[8,1,27000]{2,1,0:T(1,128)}), f32[8,1,27000]{2,1,0:T(1,128)}, u32[]{:S(2)}, u32[]{:S(2)}) async-start(f32[8,1,27000]{2,1,0:T(1,128)} %reshape.358), calls=%async_computation.2 | async-start | bytes 1728512 | tf_op jit(solution)/shard_map/all_to_all | solution.py:48
  272.8 2.8 reduce.11
  275.5 14.8 %reshape.357 = f32[14400,1,15]{2,1,0:T(1,128)} reshape(f32[8,27000]{1,0:T(8,128)S(1)} %reduce.11) | data formatting | bytes 1728000
  290.4 5.1 %copy.86 = f32[1,15,8,1800]{3,2,0,1:T(8,128)S(1)} copy(f32[1,15,8,1800]{1,3,2,0:T(8,128)} %bitcast.124) | data formatting | bytes 1728000 | tf_op jit(solution)/shard_map/all_to_all | solution.py:48
  295.8 1.4 convolution_multiply_fusion
  297.2 1.2 convolution_bitcast_fusion
  298.4 1.9 copy.71
  300.3 5.7 %all-to-all-start.5 = ((f32[1,120,1800]{2,0,1:T(1,128)}), f32[1,120,1800]{2,0,1:T(1,128)S(1)}, u32[]{:S(2)}, u32[]{:S(2)}) async-start(f32[1,120,1800]{2,0,1:T(1,128)} %copy.71), calls=%async_computation.5 | async-start | bytes 1843200 | tf_op jit(solution)/shard_map/all_to_all | solution.py:55
  306.0 3.9 %reduce.13 = f32[8,27000]{1,0:T(8,128)S(1)} reduce(f32[8,1,27000]{2,1,0:T(1,128)} %all-to-all-done.2, f32[]{:T(128)} %broadcast.280), dimensions={1}, to_apply=%all_to_all.66.reduce_sub_computation | reduce | bytes 1728004 | tf_op jit(solution)/shard_map/all_to_all | solution.py:48
  309.9 14.8 %reshape.359 = f32[14400,1,15]{2,1,0:T(1,128)} reshape(f32[8,27000]{1,0:T(8,128)S(1)} %reduce.13) | data formatting | bytes 1728000
  324.7 6.1 %copy.82 = f32[1,15,8,1800]{3,2,0,1:T(8,128)} copy(f32[1,15,8,1800]{1,3,2,0:T(8,128)} %bitcast.125) | data formatting | bytes 1728000 | tf_op jit(solution)/shard_map/all_to_all | solution.py:48
  330.9 1.4 copy.63
  332.3 1.1 reshape.315
  333.4 2.5 convolution_multiply_fusion.1
  335.9 1.2 convolution_bitcast_fusion.1
  337.1 1.9 copy.64
  339.0 5.7 %all-to-all-start.3 = ((f32[1,120,1800]{2,0,1:T(1,128)}), f32[1,120,1800]{2,0,1:T(1,128)}, u32[]{:S(2)}, u32[]{:S(2)}) async-start(f32[1,120,1800]{2,0,1:T(1,128)} %copy.64), calls=%async_computation.3 | async-start | bytes 1843200 | tf_op jit(solution)/shard_map/all_to_all | solution.py:55
  344.7 0.9 reshape.320
  345.6 1.9 fusion.14
  347.5 2.5 fusion.88
  350.0 2.8 mul.246
  352.8 2.2 fusion.7
  355.2 2.2 copy.65
  357.4 3.0 reshape.316
  360.4 3.0 fusion.18
  363.4 2.2 fusion
  365.6 2.7 mul.241
  368.4 2.5 reshape_reshape.2
  370.9 4.1 %fusion.9 = f32[1,15,14400]{2,0,1:T(1,128)} fusion(f32[1,15,14400]{2,0,1:T(1,128)} %collective-permute-done.1, f32[1,15,14400]{2,0,1:T(1,128)S(1)} %mul.241, f32[1,1,15,14400]{3,0,2,1:T(1,128)} %reshape_reshape.2, f32[2,1,15,14400]{3,0,2,1:T(2,128)S(1)} %copy-done.1), kind=kLoop, calls=%fused_computation.26 | loop fusion | flops 864000 | bytes 4320000 | tf_op jit(solution)/shard_map/mul | solution.py:123
  (37 shorter events, 1.9 us)
Async XLA Ops:
  3.9 12.3 %copy-start.3 = (s32[1,704]{1,0:T(1,128)S(1)}, s32[1,704]{1,0:T(1,128)}, u32[]{:S(2)}) copy-start(s32[1,704]{1,0:T(1,128)} %param.6) | copy-start | bytes 8452
  3.9 12.4 %copy-start.4 = (s32[1,352]{1,0:T(1,128)S(1)}, s32[1,352]{1,0:T(1,128)}, u32[]{:S(2)}) copy-start(s32[1,352]{1,0:T(1,128)} %param.8) | copy-start | bytes 4228
  5.8 26.8 %all-to-all-start = ((f32[32,1,2640]{2,1,0:T(1,128)}), f32[32,1,2640]{2,1,0:T(1,128)S(1)}, u32[]{:S(2)}, u32[]{:S(2)}) async-start(f32[32,1,2640]{2,1,0:T(1,128)} %copy.55), calls=%async_computation | async-start | bytes 688128 | tf_op jit(solution)/shard_map/all_to_all | solution.py:87
  63.9 25.8 %collective-permute-start = (f32[2,1,15,14400]{3,0,2,1:T(2,128)S(1)}, f32[2,1,15,14400]{3,0,2,1:T(2,128)S(1)}, u32[]{:S(2)}, u32[]{:S(2)}) collective-permute-start(f32[2,1,15,14400]{3,0,2,1:T(2,128)S(1)} %stack.3), channel_id=1, source_target_pairs={{0,8},{8,16},{16,24},{24,32},{32,40},{40,48},{48,56},{56,64},{64,7... | collective-permute-start | bytes 5184008 | tf_op jit(solution)/shard_map/ppermute | solution.py:21
  89.7 1.2 copy-start
  180.2 86.3 %all-to-all-start.4 = ((f32[8,1,27000]{2,1,0:T(1,128)}), f32[8,1,27000]{2,1,0:T(1,128)S(1)}, u32[]{:S(2)}, u32[]{:S(2)}) async-start(f32[8,1,27000]{2,1,0:T(1,128)} %reshape.356), calls=%async_computation.4 | async-start | bytes 1728512 | tf_op jit(solution)/shard_map/all_to_all | solution.py:48
  266.5 33.8 %all-to-all-start.2 = ((f32[8,1,27000]{2,1,0:T(1,128)}), f32[8,1,27000]{2,1,0:T(1,128)}, u32[]{:S(2)}, u32[]{:S(2)}) async-start(f32[8,1,27000]{2,1,0:T(1,128)} %reshape.358), calls=%async_computation.2 | async-start | bytes 1728512 | tf_op jit(solution)/shard_map/all_to_all | solution.py:48
  300.3 38.7 %all-to-all-start.5 = ((f32[1,120,1800]{2,0,1:T(1,128)}), f32[1,120,1800]{2,0,1:T(1,128)S(1)}, u32[]{:S(2)}, u32[]{:S(2)}) async-start(f32[1,120,1800]{2,0,1:T(1,128)} %copy.71), calls=%async_computation.5 | async-start | bytes 1843200 | tf_op jit(solution)/shard_map/all_to_all | solution.py:55
  339.0 16.2 %all-to-all-start.3 = ((f32[1,120,1800]{2,0,1:T(1,128)}), f32[1,120,1800]{2,0,1:T(1,128)}, u32[]{:S(2)}, u32[]{:S(2)}) async-start(f32[1,120,1800]{2,0,1:T(1,128)} %copy.64), calls=%async_computation.3 | async-start | bytes 1843200 | tf_op jit(solution)/shard_map/all_to_all | solution.py:55
  350.0 2.8 copy-start.1
  355.0 15.8 %collective-permute-start.1 = (f32[1,15,14400]{2,0,1:T(1,128)}, f32[1,15,14400]{2,0,1:T(1,128)}, u32[]{:S(2)}, u32[]{:S(2)}) collective-permute-start(f32[1,15,14400]{2,0,1:T(1,128)} %fusion.7), channel_id=1, source_target_pairs={{0,248},{8,0},{16,8},{24,16},{32,24},{40,32},{48,40},{56,48},{64,5... | collective-permute-start | bytes 2592008 | tf_op jit(solution)/shard_map/ppermute | solution.py:21
  365.6 2.8 copy-start.2
where the time goes:
time: 382 us; the launch traced here: 375 us
  other arithmetic  152 us (40%)
  local copies, waits for them, and re-layouts  103 us (27%)
  waiting for transfers between devices  41.2 us (11%)
  starting transfers between devices  33.8 us (9%)
  matrix products  27 us (7%)
  blocking collectives  18 us (5%)
    unnamed x5, other arithmetic  132 us
    unnamed x15, local copies, waits for them, and re-layouts  47.4 us
    ppermute x2, waiting for transfers between devices, from_behind(): return lax.ppermute(x, axis, [(i, (i + by) % count) for i in range(count)])  25.2 us
    all_to_all x1, blocking collectives, local(): lax.all_to_all(col_grid, 'fft', split_axis=1, concat_axis=2, tiled=True)  18 us
    all_to_all x1, waiting for transfers between devices, local(): lax.all_to_all(row_data, 'band', split_axis=0, concat_axis=2, tiled=True)  16 us
    all_to_all x4, local copies, waits for them, and re-layouts, potential(): lax.all_to_all(spectrum, 'fft', split_axis=2, concat_axis=1, tiled=True)  12.8 us
    dot_general x5, matrix products, planar(): jnp.einsum('pzxy,yl->pzxl', cube_view, hart_y, precision=PRECISE)  11.7 us
    all_to_all x2, starting transfers between devices, potential(): lax.all_to_all(back_z, 'fft', split_axis=1, concat_axis=2, tiled=True)  11.4 us
  transfers between devices with their start and end apart: 7, of which 2 were waited for; matrix products, arithmetic and copies ran while one was open for 45% of the time, Pallas kernels for 0%

commit v1 on v0

v1 whole, which is shorter than its diff:
```python
import math

import jax
import jax.numpy as jnp
import ml_dtypes
import numpy as np
from jax import lax
from jax.experimental import pallas as pl
from jax.experimental.pallas import tpu as pltpu
from jax.sharding import PartitionSpec as P

N = 120
NF = 8
NBAND = 32
ZL = N // NF
ZP = 16
CAP = 22
CAPP = 24
STICKS = 352
STP = 384
L = 128
BLK = ZL * ZP
COULOMB = 0.25
EXCHANGE_FRACTION = 0.25
F32 = jnp.float32
BF16 = jnp.bfloat16


def cas_parts():
    k = np.arange(N)
    angle = (k[:, None] * k[None, :] % N) * (2.0 * math.pi / N)
    full = np.cos(angle) + np.sin(angle)
    zpad = (k // ZL) * ZP + k % ZL

    def parts(a):
        hi = a.astype(ml_dtypes.bfloat16)
        lo = (a - hi.astype(np.float64)).astype(ml_dtypes.bfloat16)
        return hi, lo

    def place(rows, cols):
        out = np.zeros((L, L))
        out[np.ix_(rows, cols)] = full
        return out

    def right(a):
        hi, lo = parts(a)
        row = np.concatenate([hi, lo], axis=1)
        return np.concatenate([row, row], axis=0)

    def left(a):
        hi, lo = parts(a)
        return np.concatenate([hi, lo], axis=1)

    plain = place(k, k)
    return (
        right(plain),
        right(place(k, zpad)),
        left(plain),
        left(place(k, zpad)),
        left(place(zpad, k)),
    )


def halves(x):
    hi = x.astype(BF16)
    lo = (x - hi.astype(F32)).astype(BF16)
    return jnp.concatenate([hi, lo], axis=1)


def fold(r):
    return r[:, :L] + r[:, L:]


def dot(a, b):
    return jnp.dot(a, b, preferred_element_type=F32)


def right_mul(x, table):
    return fold(dot(halves(x), table))


def left_mul(table, x):
    cat = halves(x)
    return fold(dot(table, jnp.concatenate([cat, cat], axis=0)))


def kernel(
    coef, owned, counts, cols, order, hr, hrz, lx, lz1, lz2, out,
    stage, stage3, send1, recv1, sel, keep, owned_p, cols_p, at_send, at_recv, phi, tb, tb2,
    coul, send_f, recv_f, send_b, recv_b, send_v, recv_v, acc,
    s1, r1, s2, r2, sf, rf, sb, rb, sv, rv,
):
    band = lax.axis_index("band")
    fft = lax.axis_index("fft")
    nxt = lax.rem(band + 1, NBAND)
    prv = lax.rem(band + NBAND - 1, NBAND)

    def copy(src, dst, ssem, rsem, b, f):
        return pltpu.make_async_remote_copy(
            src_ref=src, dst_ref=dst, send_sem=ssem, recv_sem=rsem,
            device_id=(b, f), device_id_type=pl.DeviceIdType.MESH,
        )

    barrier = pltpu.get_barrier_semaphore()

    def hello_band(d, c):
        pl.semaphore_signal(
            barrier, inc=1, device_id=(lax.rem(band + d, NBAND), fft),
            device_id_type=pl.DeviceIdType.MESH)
        return c

    lax.fori_loop(1, NBAND, hello_band, 0)

    def hello_fft(d, c):
        f = lax.rem(fft + d, NF)
        pl.semaphore_signal(
            barrier, inc=1, device_id=(band, f), device_id_type=pl.DeviceIdType.MESH)
        pl.semaphore_signal(
            barrier, inc=1, device_id=(nxt, f), device_id_type=pl.DeviceIdType.MESH)
        return c

    lax.fori_loop(1, NF, hello_fft, 0)

    stage[...] = jnp.zeros(stage.shape, F32)
    for q in range(CAP):
        stage[pl.ds(q, NBAND, stride=CAPP), pl.ds(0, N)] = coef[:, N * q:N * q + N]

    stage3[...] = stage[...].reshape(NBAND, CAPP, L)

    def reorder(j, c):
        send1[j] = stage3[order[j]]
        return c

    lax.fori_loop(0, NBAND, reorder, 0)

    pl.semaphore_wait(barrier, NBAND - 1 + 2 * (NF - 1))

    def go1(d, c):
        b = lax.rem(band + d, NBAND)
        copy(send1.at[b], recv1.at[band], s1.at[b], r1.at[band], b, fft).start()
        return c

    lax.fori_loop(1, NBAND, go1, 0)
    recv1[band] = send1[band]

    tb[...] = jnp.zeros(tb.shape, F32)
    tb2[...] = jnp.zeros(tb2.shape, F32)
    owned_p[...] = jnp.full(owned_p.shape, -1, jnp.int32)
    for o in range(NBAND):
        owned_p[:, CAPP * o:CAPP * o + CAP] = owned[:, CAP * o:CAP * o + CAP]
    rows = lax.broadcasted_iota(jnp.int32, (STICKS, NBAND * CAPP), 0)
    sel[...] = jnp.where(rows == owned_p[...], 1.0, 0.0).astype(BF16)
    cols_p[...] = jnp.full(cols_p.shape, -1.0, F32)
    cols_p[0:1, 0:STICKS] = cols[...].astype(F32)
    cols_p[1:2, 0:STICKS] = counts[...].astype(F32)
    count_b = jnp.transpose(jnp.broadcast_to(cols_p[1:2, :], (L, STP)))[:STICKS]
    kz = lax.broadcasted_iota(jnp.int32, (STICKS, L), 1)
    need = (2 * jnp.minimum(kz, N - kz) + 1).astype(F32)
    keep[...] = jnp.where((kz < N) & (need <= count_b), 1.0, 0.0)
    scale = -EXCHANGE_FRACTION * COULOMB * math.sqrt(N ** 3) / N ** 3
    r0 = lax.broadcasted_iota(jnp.int32, (L, L), 0)
    r1_ = lax.broadcasted_iota(jnp.int32, (L, L), 1)
    mz = jnp.minimum(r0, N - r0)
    my = jnp.minimum(r1_, N - r1_)
    plane = mz * mz + my * my

    def coulomb(x, c):
        kx = fft * ZL + x
        mx = jnp.minimum(kx, N - kx)
        q = (plane + mx * mx).astype(F32)
        coul[x] = jnp.where(q > 0.0, scale / jnp.maximum(q, 1.0), 0.0)
        return c

    lax.fori_loop(0, ZL, coulomb, 0)

    def got1(d, c):
        b = lax.rem(band + d, NBAND)
        copy(send1.at[b], recv1.at[b], s1.at[b], r1.at[b], b, fft).wait_recv()
        return c

    lax.fori_loop(1, NBAND, got1, 0)

    arrived = halves(recv1[...].reshape(NBAND * CAPP, L))
    picked = dot(sel[...], arrived)
    kept = keep[...] > 0.0
    hi = jnp.where(kept, picked[:, :L], 0.0).astype(BF16)
    lo = jnp.where(kept, picked[:, L:], 0.0).astype(BF16)
    along = fold(dot(jnp.concatenate([hi, lo], axis=1), hrz[...]))
    along = jnp.concatenate([along, jnp.zeros((STP - STICKS, L), F32)], axis=0)
    flipped = jnp.transpose(along)
    for f in range(NF):
        at_send[f] = flipped[f * ZP:(f + 1) * ZP]
        at_send[f, ZP - 1:ZP, :] = cols_p[0:1, :]

    def go2(d, c):
        f = lax.rem(fft + d, NF)
        copy(at_send.at[f], at_recv.at[0, fft], s2.at[0, f], r2.at[0, fft], band, f).start()
        return c

    def go2n(d, c):
        f = lax.rem(fft + d, NF)
        copy(at_send.at[f], at_recv.at[1, fft], s2.at[1, f], r2.at[1, fft], prv, f).start()
        return c

    lax.fori_loop(1, NF, go2, 0)
    lax.fori_loop(0, NF, go2n, 0)
    at_recv[0, fft] = at_send[fft]

    def got2(which, f):
        copy(at_send.at[f], at_recv.at[which, f], s2.at[which, f], r2.at[which, f],
             nxt, f).wait_recv()

    lax.fori_loop(1, NF, lambda d, c: (got2(0, lax.rem(fft + d, NF)), c)[1], 0)
    lax.fori_loop(0, NF, lambda d, c: (got2(1, d), c)[1], 0)

    srow = lax.broadcasted_iota(jnp.int32, (ZP, STP), 0)
    kyrow = lax.broadcasted_iota(jnp.int32, (L, STP), 0).astype(F32)

    def orbital(which):
        def spread(f, c):
            blk = at_recv[which, f]
            col = blk[ZP - 1:ZP, :]
            kx = jnp.floor((col + 0.5) * (1.0 / N))
            ky = col - N * kx
            a = jnp.where(srow < ZL, blk, 0.0)
            hot = jnp.where(kyrow == ky, 1.0, 0.0).astype(BF16)
            a_hi = a.astype(BF16).astype(F32)
            a_lo = a - a_hi
            his, los = [], []
            for x in range(ZL):
                hit = kx == x
                his.append(jnp.where(hit, a_hi, 0.0).astype(BF16))
                los.append(jnp.where(hit, a_lo, 0.0).astype(BF16))
            w = jnp.concatenate(his + los, axis=0)
            g = lax.dot_general(w, hot, (((1,), (1,)), ((), ())),
                                preferred_element_type=F32).astype(BF16)
            g = jnp.concatenate([g[:BLK], g[BLK:]], axis=1)
            tb[pl.ds(pl.multiple_of(f * BLK, 8), BLK), :] = fold(dot(g, hr[...]))
            return c

        lax.fori_loop(0, NF, spread, 0)
        for z in range(ZL):
            phi[which, z] = left_mul(lx[...], tb[pl.ds(z, L, stride=ZP), :])

    orbital(0)
    orbital(1)

    def forward(p):
        other = 1 - p
        for z in range(ZL):
            tb[pl.ds(z, L, stride=ZP), :] = left_mul(lx[...], phi[0, z] * phi[other, z])

        def block(f):
            return right_mul(tb[pl.ds(pl.multiple_of(f * BLK, 8), BLK), :], hr[...])

        def go(d, c):
            f = lax.rem(fft + d, NF)
            send_f[p, f] = block(f)
            copy(send_f.at[p, f], recv_f.at[p, fft], sf.at[p, f], rf.at[p, fft],
                 band, f).start()
            return c

        lax.fori_loop(1, NF, go, 0)
        recv_f[p, fft] = block(fft)

    def solve(p):
        def got(d, c):
            f = lax.rem(fft + d, NF)
            copy(send_f.at[p, f], recv_f.at[p, f], sf.at[p, f], rf.at[p, f],
                 band, f).wait_recv()
            return c

        lax.fori_loop(1, NF, got, 0)
        for x in range(ZL):
            data = recv_f[p, :, x * ZP:(x + 1) * ZP, :].reshape(L, L)
            spec = left_mul(lz1[...], data) * coul[x]
            back = left_mul(lz2[...], spec)
            send_b[p, :, x * ZP:(x + 1) * ZP, :] = back.reshape(NF, ZP, L)

        def go(d, c):
            f = lax.rem(fft + d, NF)
            copy(send_b.at[p, f], recv_b.at[p, fft], sb.at[p, f], rb.at[p, fft],
                 band, f).start()
            return c

        lax.fori_loop(1, NF, go, 0)
        recv_b[p, fft] = send_b[p, fft]

    def backward(p):
        def got(d, c):
            f = lax.rem(fft + d, NF)
            @pl.when(d > 0)
            def _():
                copy(send_b.at[p, f], recv_b.at[p, f], sb.at[p, f], rb.at[p, f],
                     band, f).wait_recv()
            tb2[pl.ds(pl.multiple_of(f * BLK, 8), BLK), :] = right_mul(recv_b[p, f], hr[...])
            return c

        lax.fori_loop(0, NF, got, 0)

    forward(0)
    forward(1)
    solve(0)
    solve(1)
    backward(0)
    for z in range(ZL):
        v = left_mul(lx[...], tb2[pl.ds(z, L, stride=ZP), :])
        acc[z] = (v * phi[1, z])[:N]
        send_v[z] = (v * phi[0, z])[:N]
    to_next = copy(send_v, recv_v, sv, rv, nxt, fft)
    to_next.start()
    backward(1)
    to_next.wait_recv()
    for z in range(ZL):
        v = left_mul(lx[...], tb2[pl.ds(z, L, stride=ZP), :])
        res = (v * phi[0, z])[:N] + acc[z] + recv_v[z]
        tb[pl.ds(z, N, stride=ZP), :] = res

    lane = lax.broadcasted_iota(jnp.int32, (ZP, L), 1)
    total = N * N
    for t in range(-(-total // L)):
        x, off = divmod(t * L, N)
        val = tb[x * ZP:(x + 1) * ZP, :]
        if off:
            val = pltpu.roll(val, L - off, 1)
        if x + 1 < N:
            more = pltpu.roll(tb[(x + 1) * ZP:(x + 2) * ZP, :], N - off, 1)
            val = jnp.where(lane < N - off, val, more)
        width = min(L, total - t * L)
        out[:, t * L:t * L + width] = val[:ZL, :width]

    def left1(d, c):
        b = lax.rem(band + d, NBAND)
        copy(send1.at[b], recv1.at[b], s1.at[b], r1.at[b], b, fft).wait_send()
        return c

    lax.fori_loop(1, NBAND, left1, 0)

    def left2(d, c):
        f = lax.rem(fft + d, NF)
        copy(at_send.at[f], at_recv.at[0, f], s2.at[0, f], r2.at[0, f], band, f).wait_send()
        for p in range(2):
            copy(send_f.at[p, f], recv_f.at[p, f], sf.at[p, f], rf.at[p, f],
                 band, f).wait_send()
            copy(send_b.at[p, f], recv_b.at[p, f], sb.at[p, f], rb.at[p, f],
                 band, f).wait_send()
        return c

    lax.fori_loop(1, NF, left2, 0)

    def left2n(f, c):
        copy(at_send.at[f], at_recv.at[1, f], s2.at[1, f], r2.at[1, f], prv, f).wait_send()
        return c

    lax.fori_loop(0, NF, left2n, 0)
    to_next.wait_send()


def local(coefficients, owned_sticks, stick_counts, stick_columns, band_order):
    tables = [jnp.asarray(t) for t in cas_parts()]
    vmem = pl.BlockSpec(memory_space=pltpu.VMEM)
    dma = pltpu.SemaphoreType.DMA
    out = pl.pallas_call(
        kernel,
        out_shape=jax.ShapeDtypeStruct((ZL, N * N), F32),
        in_specs=[vmem] * 4 + [pl.BlockSpec(memory_space=pltpu.SMEM)] + [vmem] * 5,
        out_specs=vmem,
        scratch_shapes=[
            pltpu.VMEM((NBAND * CAPP, L), F32),
            pltpu.VMEM((NBAND, CAPP, L), F32),
            pltpu.VMEM((NBAND, CAPP, L), F32),
            pltpu.VMEM((NBAND, CAPP, L), F32),
            pltpu.VMEM((STICKS, NBAND * CAPP), BF16),
            pltpu.VMEM((STICKS, L), F32),
            pltpu.VMEM((1, NBAND * CAPP), jnp.int32),
            pltpu.VMEM((8, STP), F32),
            pltpu.VMEM((NF, ZP, STP), F32),
            pltpu.VMEM((2, NF, ZP, STP), F32),
            pltpu.VMEM((2, ZL, L, L), F32),
            pltpu.VMEM((L * ZP, L), F32),
            pltpu.VMEM((L * ZP, L), F32),
            pltpu.VMEM((ZL, L, L), F32),
            pltpu.VMEM((2, NF, BLK, L), F32),
            pltpu.VMEM((2, NF, BLK, L), F32),
            pltpu.VMEM((2, NF, BLK, L), F32),
            pltpu.VMEM((2, NF, BLK, L), F32),
            pltpu.VMEM((ZL, N, L), F32),
            pltpu.VMEM((ZL, N, L), F32),
            pltpu.VMEM((ZL, N, L), F32),
            dma((NBAND,)), dma((NBAND,)),
            dma((2, NF)), dma((2, NF)),
            dma((2, NF)), dma((2, NF)),
            dma((2, NF)), dma((2, NF)),
            dma, dma,
        ],
        compiler_params=pltpu.CompilerParams(
            collective_id=0, has_side_effects=True, vmem_limit_bytes=48 * 1024 * 1024),
    )(coefficients, owned_sticks, stick_counts, stick_columns, band_order, *tables)
    return out[None]


def solution(mesh):
    placed = (P(None, ("band", "fft")), P("fft", None), P("fft", None), P("fft", None), P())
    return jax.shard_map(
        local, mesh=mesh, in_specs=placed, out_specs=P("band", "fft", None), check_vma=False
    )
```

time: 382 us -> 105 us (0.27); the launches traced: 375 us -> 105 us
  other arithmetic: 152 us -> 0 us
  Pallas kernels: 0 us -> 94.9 us
  local copies, waits for them, and re-layouts: 103 us -> 9.8 us
  waiting for transfers between devices: 41.2 us -> 0 us
  starting transfers between devices: 33.8 us -> 0 us
  matrix products: 27 us -> 0 us
  blocking collectives: 18 us -> 0 us
    unnamed x5 -> x0, other arithmetic: 132 us -> none
    pallas_call x0 -> x1, Pallas kernels: none -> 94.9 us  [local(): pl.pallas_call(kernel, out_shape=jax.ShapeDtypeStruct((ZL, N * N), F32),...]
    unnamed x15 -> x20, local copies, waits for them, and re-layouts: 47.4 us -> 8 us
    all_to_all x5 -> x0, starting transfers between devices: 33 us -> none  [the longest x2 11.4 us: potential(): lax.all_to_all(back_z, 'fft', split_axis=1, concat_axis=2, tiled=True)]
    dot_general x15 -> x0, matrix products: 27 us -> none  [the longest x5 11.7 us: planar(): jnp.einsum('pzxy,yl->pzxl', cube_view, hart_y, precision=PRECISE)]
    ppermute x2 -> x0, waiting for transfers between devices: 25.2 us -> none  [from_behind(): return lax.ppermute(x, axis, [(i, (i + by) % count) for i in range(count)])]
    all_to_all x1 -> x0, blocking collectives: 18 us -> none  [local(): lax.all_to_all(col_grid, 'fft', split_axis=1, concat_axis=2, tiled=True)]
    all_to_all x5 -> x0, waiting for transfers between devices: 16 us -> none  [the longest x1 16 us: local(): lax.all_to_all(row_data, 'band', split_axis=0, concat_axis=2, tiled=True)]
  transfers between devices with their start and end apart: 7 -> 0, of which waited for: 2 -> 0; matrix products, arithmetic and copies ran while one was open for 45% -> 0% of each run, Pallas kernels for 0% -> 0%
where the time goes in v1:
time: 105 us
  Pallas kernels  94.9 us (90%)
  local copies, waits for them, and re-layouts  9.8 us (9%)
    pallas_call x1, Pallas kernels, local(): pl.pallas_call(kernel, out_shape=jax.ShapeDtypeStruct((ZL, N * N), F32),...  94.9 us
    unnamed x20, local copies, waits for them, and re-layouts  8 us

profile of v1, /device:TPU:2, one launch (start us, length us, event | category | flops | bytes accessed | tf_op | source)
XLA Modules:
  0.0 104.7 jit_solution(5946677929073458912)
XLA Ops:
  0.0 0.0 copy-start
  0.0 1.0 copy-done
  1.0 0.0 copy-start.1
  1.0 0.9 copy-done.1
  1.9 0.0 copy-start.2
  1.9 0.9 copy-done.2
  2.8 0.0 copy-start.3
  2.8 0.8 copy-done.3
  3.6 0.0 copy-start.4
  3.6 0.8 copy-done.4
  4.5 0.0 copy-start.5
  4.5 0.8 copy-done.5
  5.3 0.0 copy-start.6
  5.3 0.7 copy-done.6
  6.0 0.0 copy-start.7
  6.0 0.7 copy-done.7
  6.7 0.0 copy-start.8
  6.7 0.7 copy-done.8
  7.4 0.0 copy-start.9
  7.4 0.7 copy-done.9
  8.0 94.9 %shard_map.100 = f32[15,14400]{1,0:T(8,128)S(1)} custom-call(f32[32,2640]{1,0:T(8,128)S(1)} %copy-done, s32[1,704]{1,0:T(1,128)S(1)} %copy-done.6, s32[1,352]{1,0:T(1,128)S(1)} %copy-done.7, s32[1,352]{1,0:T(1,128)S(1)} %copy-done.8, s32[32]{0:T(128)S(1)} %copy-done.9, bf16[256,256]{1,0:T(8,128)(2,1)S(1)} %copy-done.2, bf16[256,256]{1,0:T(8,128)(2,1)S(1)} %copy-done.1, ...), custom_call_target="tpu_custom_call" | custom-call | tf_op jit(solution)/shard_map/pallas_call | solution.py:363
  102.9 1.8 %copy.11 = f32[1,15,14400]{2,0,1:T(1,128)} copy(f32[1,15,14400]{2,1,0:T(8,128)S(1)} %bitcast.1) | data formatting | bytes 1728000 | tf_op jit(solution)/shard_map/broadcast_in_dim | solution.py:399
Async XLA Ops:
  0.0 1.0 copy-start
  1.0 0.9 copy-start.1
  1.9 0.9 copy-start.2
  2.8 0.8 copy-start.3
  3.6 0.8 copy-start.4
  4.5 0.8 copy-start.5
  5.3 0.7 copy-start.6
  6.0 0.7 copy-start.7
  6.7 0.7 copy-start.8
  7.4 0.7 copy-start.9

commit v2 on v1

--- a/solution.py
+++ b/solution.py
@@ -20,6 +20,9 @@
 STP = 384
 L = 128
 BLK = ZL * ZP
+CHUNK = 5
+ROUTES = ((0, 4, 6), (4, 4, 1), (8, 4, 7), (12, 3, 0))
+EARLY = 5
 COULOMB = 0.25
 EXCHANGE_FRACTION = 0.25
 F32 = jnp.float32
@@ -52,13 +55,12 @@
         return np.concatenate([hi, lo], axis=1)
 
     plain = place(k, k)
-    return (
+    return np.concatenate([
         right(plain),
         right(place(k, zpad)),
         left(plain),
-        left(place(k, zpad)),
         left(place(zpad, k)),
-    )
+    ], axis=0)
 
 
 def halves(x):
@@ -85,11 +87,16 @@
 
 
 def kernel(
-    coef, owned, counts, cols, order, hr, hrz, lx, lz1, lz2, out,
+    coef_h, owned_h, counts_h, cols_h, order_h, tables_h, out,
+    coef, owned, counts, cols, order, tables,
     stage, stage3, send1, recv1, sel, keep, owned_p, cols_p, at_send, at_recv, phi, tb, tb2,
-    coul, send_f, recv_f, send_b, recv_b, send_v, recv_v, acc,
-    s1, r1, s2, r2, sf, rf, sb, rb, sv, rv,
+    coul, send_f, recv_f3, send_b, recv_b, send_v, recv_v, acc, relay,
+    s1, r1, s2, r2, sf, rf, sb, rb, sv, rv, rr, sr, sin,
 ):
+    hr = tables.at[0:2 * L]
+    hrz = tables.at[2 * L:4 * L]
+    lx = tables.at[4 * L:5 * L]
+    lp = tables.at[5 * L:6 * L]
     band = lax.axis_index("band")
     fft = lax.axis_index("fft")
     nxt = lax.rem(band + 1, NBAND)
@@ -101,6 +108,8 @@
             device_id=(b, f), device_id_type=pl.DeviceIdType.MESH,
         )
 
+    recv_f = recv_f3.reshape(2, L * ZP, L)
+
     barrier = pltpu.get_barrier_semaphore()
 
     def hello_band(d, c):
@@ -115,25 +124,35 @@
         f = lax.rem(fft + d, NF)
         pl.semaphore_signal(
             barrier, inc=1, device_id=(band, f), device_id_type=pl.DeviceIdType.MESH)
-        pl.semaphore_signal(
-            barrier, inc=1, device_id=(nxt, f), device_id_type=pl.DeviceIdType.MESH)
         return c
 
     lax.fori_loop(1, NF, hello_fft, 0)
 
+    loads = [
+        pltpu.make_async_copy(src, dst, sin.at[n])
+        for n, (src, dst) in enumerate([
+            (coef_h, coef), (order_h, order), (owned_h, owned), (counts_h, counts),
+            (cols_h, cols), (tables_h, tables)])
+    ]
+    for load in loads:
+        load.start()
+
     stage[...] = jnp.zeros(stage.shape, F32)
+    loads[0].wait()
     for q in range(CAP):
         stage[pl.ds(q, NBAND, stride=CAPP), pl.ds(0, N)] = coef[:, N * q:N * q + N]
 
     stage3[...] = stage[...].reshape(NBAND, CAPP, L)
 
+    loads[1].wait()
+
     def reorder(j, c):
         send1[j] = stage3[order[j]]
         return c
 
     lax.fori_loop(0, NBAND, reorder, 0)
 
-    pl.semaphore_wait(barrier, NBAND - 1 + 2 * (NF - 1))
+    pl.semaphore_wait(barrier, NBAND - 1 + NF - 1)
 
     def go1(d, c):
         b = lax.rem(band + d, NBAND)
@@ -144,7 +163,11 @@
     recv1[band] = send1[band]
 
     tb[...] = jnp.zeros(tb.shape, F32)
-    tb2[...] = jnp.zeros(tb2.shape, F32)
+    tb2[N * ZP:, :] = jnp.zeros(((L - N) * ZP, L), F32)
+    for p in range(2):
+        recv_f[p, N * ZP:, :] = jnp.zeros(((L - N) * ZP, L), F32)
+    for load in loads[2:]:
+        load.wait()
     owned_p[...] = jnp.full(owned_p.shape, -1, jnp.int32)
     for o in range(NBAND):
         owned_p[:, CAPP * o:CAPP * o + CAP] = owned[:, CAP * o:CAP * o + CAP]
@@ -197,27 +220,28 @@
         copy(at_send.at[f], at_recv.at[0, fft], s2.at[0, f], r2.at[0, fft], band, f).start()
         return c
 
-    def go2n(d, c):
-        f = lax.rem(fft + d, NF)
-        copy(at_send.at[f], at_recv.at[1, fft], s2.at[1, f], r2.at[1, fft], prv, f).start()
-        return c
-
     lax.fori_loop(1, NF, go2, 0)
-    lax.fori_loop(0, NF, go2n, 0)
     at_recv[0, fft] = at_send[fft]
-
-    def got2(which, f):
-        copy(at_send.at[f], at_recv.at[which, f], s2.at[which, f], r2.at[which, f],
-             nxt, f).wait_recv()
-
-    lax.fori_loop(1, NF, lambda d, c: (got2(0, lax.rem(fft + d, NF)), c)[1], 0)
-    lax.fori_loop(0, NF, lambda d, c: (got2(1, d), c)[1], 0)
 
     srow = lax.broadcasted_iota(jnp.int32, (ZP, STP), 0)
     kyrow = lax.broadcasted_iota(jnp.int32, (L, STP), 0).astype(F32)
 
+    def arrive(which, d, f):
+        if which == 0:
+            @pl.when(d > 0)
+            def _():
+                copy(at_send.at[f], at_recv.at[0, f], s2.at[0, f], r2.at[0, f],
+                     band, f).wait_recv()
+            copy(at_recv.at[0, f], at_recv.at[1, f], s2.at[1, f], r2.at[1, f],
+                 prv, fft).start()
+        else:
+            copy(at_recv.at[0, f], at_recv.at[1, f], s2.at[1, f], r2.at[1, f],
+                 prv, fft).wait_recv()
+
     def orbital(which):
-        def spread(f, c):
+        def spread(d, c):
+            f = lax.rem(fft + d, NF)
+            arrive(which, d, f)
             blk = at_recv[which, f]
             col = blk[ZP - 1:ZP, :]
             kx = jnp.floor((col + 0.5) * (1.0 / N))
@@ -239,82 +263,118 @@
             return c
 
         lax.fori_loop(0, NF, spread, 0)
+        p = 1 - which
         for z in range(ZL):
-            phi[which, z] = left_mul(lx[...], tb[pl.ds(z, L, stride=ZP), :])
-
-    orbital(0)
-    orbital(1)
-
-    def forward(p):
-        other = 1 - p
-        for z in range(ZL):
-            tb[pl.ds(z, L, stride=ZP), :] = left_mul(lx[...], phi[0, z] * phi[other, z])
-
-        def block(f):
-            return right_mul(tb[pl.ds(pl.multiple_of(f * BLK, 8), BLK), :], hr[...])
-
+            value = left_mul(lx[...], tb[pl.ds(z, L, stride=ZP), :])
+            phi[which, z] = value
+            rho = left_mul(lp[...], value * (value if p else phi[0, z]))
+            rho = right_mul(rho, hr[...])
+            send_f[p, :, z] = rho.reshape(NF, ZP, L)
+            if z % CHUNK == CHUNK - 1:
+                first = z - CHUNK + 1
+
+                def go(d, c):
+                    f = lax.rem(fft + d, NF)
+                    copy(send_f.at[p, f, first:first + CHUNK],
+                         recv_f3.at[p, pl.ds(fft * ZL + first, CHUNK)],
+                         sf.at[p, f], rf.at[p, fft], band, f).start()
+                    return c
+
+                lax.fori_loop(1, NF, go, 0)
+        recv_f3[p, pl.ds(fft * ZL, ZL)] = send_f[p, fft]
+
+    def solve(p, upto):
+        def got(d, c):
+            f = lax.rem(fft + d, NF)
+            copy(send_f.at[p, f], recv_f3.at[p, pl.ds(f * ZL, ZL)],
+                 sf.at[p, f], rf.at[p, f], band, f).wait_recv()
+            return c
+
+        lax.fori_loop(1, NF, got, 0)
+        for x in range(ZL):
+            data = recv_f[p, pl.ds(x, L, stride=ZP), :]
+            spec = left_mul(lx[...], data) * coul[x]
+            send_b[p, :, x] = left_mul(lp[...], spec).reshape(NF, ZP, L)
+            if x % CHUNK == CHUNK - 1 and x < upto:
+                give(p, x - CHUNK + 1)
+
+    def give(p, first):
         def go(d, c):
             f = lax.rem(fft + d, NF)
-            send_f[p, f] = block(f)
-            copy(send_f.at[p, f], recv_f.at[p, fft], sf.at[p, f], rf.at[p, fft],
-                 band, f).start()
+            copy(send_b.at[p, f, first:first + CHUNK],
+                 recv_b.at[p, fft, first:first + CHUNK],
+                 sb.at[p, f], rb.at[p, fft], band, f).start()
             return c
 
         lax.fori_loop(1, NF, go, 0)
-        recv_f[p, fft] = block(fft)
-
-    def solve(p):
-        def got(d, c):
-            f = lax.rem(fft + d, NF)
-            copy(send_f.at[p, f], recv_f.at[p, f], sf.at[p, f], rf.at[p, f],
-                 band, f).wait_recv()
-            return c
-
-        lax.fori_loop(1, NF, got, 0)
-        for x in range(ZL):
-            data = recv_f[p, :, x * ZP:(x + 1) * ZP, :].reshape(L, L)
-            spec = left_mul(lz1[...], data) * coul[x]
-            back = left_mul(lz2[...], spec)
-            send_b[p, :, x * ZP:(x + 1) * ZP, :] = back.reshape(NF, ZP, L)
-
-        def go(d, c):
-            f = lax.rem(fft + d, NF)
-            copy(send_b.at[p, f], recv_b.at[p, fft], sb.at[p, f], rb.at[p, fft],
-                 band, f).start()
-            return c
-
-        lax.fori_loop(1, NF, go, 0)
-        recv_b[p, fft] = send_b[p, fft]
 
     def backward(p):
         def got(d, c):
             f = lax.rem(fft + d, NF)
-            @pl.when(d > 0)
+            copy(send_b.at[p, f], recv_b.at[p, f], sb.at[p, f], rb.at[p, f],
+                 band, f).wait_recv()
+            tb2[pl.ds(pl.multiple_of(f * BLK, 8), BLK), :] = right_mul(
+                recv_b[p, f].reshape(BLK, L), hr[...])
+            return c
+
+        tb2[pl.ds(pl.multiple_of(fft * BLK, 8), BLK), :] = right_mul(
+            send_b[p, fft].reshape(BLK, L), hr[...])
+        lax.fori_loop(1, NF, got, 0)
+
+    orbital(0)
+    orbital(1)
+    solve(1, EARLY)
+    solve(0, ZL)
+    for first in range(EARLY, ZL, CHUNK):
+        give(1, first)
+    backward(0)
+    far = lax.rem(band, 16) == 15
+    nxt_row = (nxt // 16) * 16
+
+    def to_next(first, count):
+        return copy(send_v.at[pl.ds(first, count)], recv_v.at[pl.ds(first, count)],
+                    sv, rv, nxt, fft)
+
+    def to_relay(first, count, hop):
+        return copy(send_v.at[pl.ds(first, count)], relay.at[pl.ds(0, count)],
+                    sv, rr, nxt_row + 2 * hop, fft)
+
+    def from_relay(first, count):
+        return copy(relay.at[pl.ds(0, count)], recv_v.at[pl.ds(first, count)],
+                    sr, rv, (band // 16) * 16, fft)
+
+    def send_term(first, count, hop):
+        if hop == 0:
+            to_next(first, count).start()
+        else:
+            @pl.when(far)
             def _():
-                copy(send_b.at[p, f], recv_b.at[p, f], sb.at[p, f], rb.at[p, f],
-                     band, f).wait_recv()
-            tb2[pl.ds(pl.multiple_of(f * BLK, 8), BLK), :] = right_mul(recv_b[p, f], hr[...])
-            return c
-
-        lax.fori_loop(0, NF, got, 0)
-
-    forward(0)
-    forward(1)
-    solve(0)
-    solve(1)
-    backward(0)
+                to_relay(first, count, hop).start()
+
+            @pl.when(jnp.logical_not(far))
+            def _():
+                to_next(first, count).start()
+
+    for first, count, hop in ROUTES:
+        for z in range(first, first + count):
+            v = left_mul(lx[...], tb2[pl.ds(z, L, stride=ZP), :])
+            acc[z] = (v * phi[1, z])[:N]
+            send_v[z] = (v * phi[0, z])[:N]
+        send_term(first, count, hop)
+    for first, count, hop in ROUTES:
+        if hop:
+            @pl.when(lax.rem(band, 16) == 2 * hop)
+            def _():
+                to_relay(first, count, hop).wait_recv()
+                from_relay(first, count).start()
+
+    backward(1)
     for z in range(ZL):
         v = left_mul(lx[...], tb2[pl.ds(z, L, stride=ZP), :])
-        acc[z] = (v * phi[1, z])[:N]
-        send_v[z] = (v * phi[0, z])[:N]
-    to_next = copy(send_v, recv_v, sv, rv, nxt, fft)
-    to_next.start()
-    backward(1)
-    to_next.wait_recv()
+        acc[z] += (v * phi[0, z])[:N]
+    to_next(0, ZL).wait_recv()
     for z in range(ZL):
-        v = left_mul(lx[...], tb2[pl.ds(z, L, stride=ZP), :])
-        res = (v * phi[0, z])[:N] + acc[z] + recv_v[z]
-        tb[pl.ds(z, N, stride=ZP), :] = res
+        tb[pl.ds(z, N, stride=ZP), :] = acc[z] + recv_v[z]
 
     lane = lax.broadcasted_iota(jnp.int32, (ZP, L), 1)
     total = N * N
@@ -327,7 +387,7 @@
             more = pltpu.roll(tb[(x + 1) * ZP:(x + 2) * ZP, :], N - off, 1)
             val = jnp.where(lane < N - off, val, more)
         width = min(L, total - t * L)
-        out[:, t * L:t * L + width] = val[:ZL, :width]
+        out[:, 0, t * L:t * L + width] = val[:ZL, :width]
 
     def left1(d, c):
         b = lax.rem(band + d, NBAND)
@@ -340,7 +400,7 @@
         f = lax.rem(fft + d, NF)
         copy(at_send.at[f], at_recv.at[0, f], s2.at[0, f], r2.at[0, f], band, f).wait_send()
         for p in range(2):
-            copy(send_f.at[p, f], recv_f.at[p, f], sf.at[p, f], rf.at[p, f],
+            copy(send_f.at[p, f], recv_f3.at[p, pl.ds(f * ZL, ZL)], sf.at[p, f], rf.at[p, f],
                  band, f).wait_send()
             copy(send_b.at[p, f], recv_b.at[p, f], sb.at[p, f], rb.at[p, f],
                  band, f).wait_send()
@@ -349,23 +409,35 @@
     lax.fori_loop(1, NF, left2, 0)
 
     def left2n(f, c):
-        copy(at_send.at[f], at_recv.at[1, f], s2.at[1, f], r2.at[1, f], prv, f).wait_send()
+        copy(at_recv.at[0, f], at_recv.at[1, f], s2.at[1, f], r2.at[1, f],
+             prv, fft).wait_send()
         return c
 
     lax.fori_loop(0, NF, left2n, 0)
-    to_next.wait_send()
+    to_next(0, ZL).wait_send()
+    for first, count, hop in ROUTES:
+        if hop:
+            @pl.when(lax.rem(band, 16) == 2 * hop)
+            def _():
+                from_relay(first, count).wait_send()
 
 
 def local(coefficients, owned_sticks, stick_counts, stick_columns, band_order):
-    tables = [jnp.asarray(t) for t in cas_parts()]
+    tables = jnp.asarray(cas_parts())
     vmem = pl.BlockSpec(memory_space=pltpu.VMEM)
     dma = pltpu.SemaphoreType.DMA
     out = pl.pallas_call(
         kernel,
-        out_shape=jax.ShapeDtypeStruct((ZL, N * N), F32),
-        in_specs=[vmem] * 4 + [pl.BlockSpec(memory_space=pltpu.SMEM)] + [vmem] * 5,
+        out_shape=jax.ShapeDtypeStruct((ZL, 1, N * N), F32),
+        in_specs=[pl.BlockSpec(memory_space=pltpu.HBM)] * 6,
         out_specs=vmem,
         scratch_shapes=[
+            pltpu.VMEM((NBAND, CAP * N), F32),
+            pltpu.VMEM((1, NBAND * CAP), jnp.int32),
+            pltpu.VMEM((1, STICKS), jnp.int32),
+            pltpu.VMEM((1, STICKS), jnp.int32),
+            pltpu.SMEM((NBAND,), jnp.int32),
+            pltpu.VMEM((6 * L, 2 * L), BF16),
             pltpu.VMEM((NBAND * CAPP, L), F32),
             pltpu.VMEM((NBAND, CAPP, L), F32),
             pltpu.VMEM((NBAND, CAPP, L), F32),
@@ -380,23 +452,25 @@
             pltpu.VMEM((L * ZP, L), F32),
             pltpu.VMEM((L * ZP, L), F32),
             pltpu.VMEM((ZL, L, L), F32),
-            pltpu.VMEM((2, NF, BLK, L), F32),
-            pltpu.VMEM((2, NF, BLK, L), F32),
-            pltpu.VMEM((2, NF, BLK, L), F32),
-            pltpu.VMEM((2, NF, BLK, L), F32),
+            pltpu.VMEM((2, NF, ZL, ZP, L), F32),
+            pltpu.VMEM((2, L, ZP, L), F32),
+            pltpu.VMEM((2, NF, ZL, ZP, L), F32),
+            pltpu.VMEM((2, NF, ZL, ZP, L), F32),
             pltpu.VMEM((ZL, N, L), F32),
             pltpu.VMEM((ZL, N, L), F32),
             pltpu.VMEM((ZL, N, L), F32),
+            pltpu.VMEM((4, N, L), F32),
             dma((NBAND,)), dma((NBAND,)),
             dma((2, NF)), dma((2, NF)),
             dma((2, NF)), dma((2, NF)),
             dma((2, NF)), dma((2, NF)),
-            dma, dma,
+            dma, dma, dma, dma,
+            dma((6,)),
         ],
         compiler_params=pltpu.CompilerParams(
-            collective_id=0, has_side_effects=True, vmem_limit_bytes=48 * 1024 * 1024),
-    )(coefficients, owned_sticks, stick_counts, stick_columns, band_order, *tables)
-    return out[None]
+            collective_id=0, has_side_effects=True, vmem_limit_bytes=60 * 1024 * 1024),
+    )(coefficients, owned_sticks, stick_counts, stick_columns, band_order, tables)
+    return out.reshape(1, ZL, N * N)
 
 
 def solution(mesh):

time: 105 us -> 91 us (0.87)
  local copies, waits for them, and re-layouts: 9.8 us -> 2.13 us
  Pallas kernels: 94.9 us -> 88.4 us
    pallas_call x1, Pallas kernels: 94.9 us -> 88.4 us  [local(): pl.pallas_call(kernel, out_shape=jax.ShapeDtypeStruct((ZL, 1, N * N), F32...]
    unnamed x20 -> x1, local copies, waits for them, and re-layouts: 8 us -> 2.13 us
    broadcast_in_dim x1 -> x0, local copies, waits for them, and re-layouts: 1.8 us -> none  [local(): return out[None]]
where the time goes in v2:
time: 91 us; the launch traced here: 90.6 us
  Pallas kernels  88.4 us (97%)
  local copies, waits for them, and re-layouts  2.13 us (2%)
    pallas_call x1, Pallas kernels, local(): pl.pallas_call(kernel, out_shape=jax.ShapeDtypeStruct((ZL, 1, N * N), F32...  88.4 us
    unnamed x1, local copies, waits for them, and re-layouts  2.13 us

profile of v2, /device:TPU:2, one launch (start us, length us, event | category | flops | bytes accessed | tf_op | source)
XLA Modules:
  0.0 90.6 jit_solution(9618285784642878093)
XLA Ops:
  0.0 88.4 %shard_map.64 = f32[15,1,14400]{2,1,0:T(1,128)} custom-call(f32[32,2640]{1,0:T(8,128)} %coef_h.1, s32[1,704]{1,0:T(1,128)} %owned_h.1, s32[1,352]{1,0:T(1,128)} %counts_h.1, s32[1,352]{1,0:T(1,128)} %cols_h.1, s32[32]{0:T(128)} %order_h.1, bf16[768,256]{1,0:T(8,128)(2,1)} %constant.2.clone.tables_h), custom_call_target="tpu_custom_call" | custom-call | tf_op jit(solution)/shard_map/pallas_call | solution.py:429
  88.4 2.1 %copy.8 = f32[1,15,14400]{2,0,1:T(1,128)} copy(f32[1,15,14400]{2,0,1:T(1,128)} %bitcast.1) | data formatting | bytes 1728000

commit v3 on v2

--- a/solution.py
+++ b/solution.py
@@ -21,8 +21,8 @@
 L = 128
 BLK = ZL * ZP
 CHUNK = 5
+PARTS = ZL // CHUNK
 ROUTES = ((0, 4, 6), (4, 4, 1), (8, 4, 7), (12, 3, 0))
-EARLY = 5
 COULOMB = 0.25
 EXCHANGE_FRACTION = 0.25
 F32 = jnp.float32
@@ -89,9 +89,9 @@
 def kernel(
     coef_h, owned_h, counts_h, cols_h, order_h, tables_h, out,
     coef, owned, counts, cols, order, tables,
-    stage, stage3, send1, recv1, sel, keep, owned_p, cols_p, at_send, at_recv, phi, tb, tb2,
+    stage, stage3, send1, recv1, sel, keep, owned_p, row_p, all_cols, kx_of, along_y, at_send, at_recv, phi, tb, tb2,
     coul, send_f, recv_f3, send_b, recv_b, send_v, recv_v, acc, relay,
-    s1, r1, s2, r2, sf, rf, sb, rb, sv, rv, rr, sr, sin,
+    sk, rk, s1, r1, s2, r2, sp, rf, rb, sv, rv, rr, sr, sin,
 ):
     hr = tables.at[0:2 * L]
     hrz = tables.at[2 * L:4 * L]
@@ -124,6 +124,8 @@
         f = lax.rem(fft + d, NF)
         pl.semaphore_signal(
             barrier, inc=1, device_id=(band, f), device_id_type=pl.DeviceIdType.MESH)
+        pl.semaphore_signal(
+            barrier, inc=1, device_id=(nxt, f), device_id_type=pl.DeviceIdType.MESH)
         return c
 
     lax.fori_loop(1, NF, hello_fft, 0)
@@ -152,7 +154,17 @@
 
     lax.fori_loop(0, NBAND, reorder, 0)
 
-    pl.semaphore_wait(barrier, NBAND - 1 + NF - 1)
+    pl.semaphore_wait(barrier, NBAND - 1 + 2 * (NF - 1))
+
+    loads[4].wait()
+    all_cols[fft] = cols[...]
+
+    def go0(d, c):
+        f = lax.rem(fft + d, NF)
+        copy(cols, all_cols.at[fft], sk.at[f], rk.at[fft], band, f).start()
+        return c
+
+    lax.fori_loop(1, NF, go0, 0)
 
     def go1(d, c):
         b = lax.rem(band + d, NBAND)
@@ -166,17 +178,16 @@
     tb2[N * ZP:, :] = jnp.zeros(((L - N) * ZP, L), F32)
     for p in range(2):
         recv_f[p, N * ZP:, :] = jnp.zeros(((L - N) * ZP, L), F32)
-    for load in loads[2:]:
-        load.wait()
+    for n in (2, 3, 5):
+        loads[n].wait()
     owned_p[...] = jnp.full(owned_p.shape, -1, jnp.int32)
     for o in range(NBAND):
         owned_p[:, CAPP * o:CAPP * o + CAP] = owned[:, CAP * o:CAP * o + CAP]
     rows = lax.broadcasted_iota(jnp.int32, (STICKS, NBAND * CAPP), 0)
     sel[...] = jnp.where(rows == owned_p[...], 1.0, 0.0).astype(BF16)
-    cols_p[...] = jnp.full(cols_p.shape, -1.0, F32)
-    cols_p[0:1, 0:STICKS] = cols[...].astype(F32)
-    cols_p[1:2, 0:STICKS] = counts[...].astype(F32)
-    count_b = jnp.transpose(jnp.broadcast_to(cols_p[1:2, :], (L, STP)))[:STICKS]
+    row_p[...] = jnp.full(row_p.shape, -1.0, F32)
+    row_p[0:1, 0:STICKS] = counts[...].astype(F32)
+    count_b = jnp.transpose(jnp.broadcast_to(row_p[0:1, :], (L, STP)))[:STICKS]
     kz = lax.broadcasted_iota(jnp.int32, (STICKS, L), 1)
     need = (2 * jnp.minimum(kz, N - kz) + 1).astype(F32)
     keep[...] = jnp.where((kz < N) & (need <= count_b), 1.0, 0.0)
@@ -195,6 +206,26 @@
         return c
 
     lax.fori_loop(0, ZL, coulomb, 0)
+
+    def got0(d, c):
+        f = lax.rem(fft + d, NF)
+        copy(cols, all_cols.at[f], sk.at[f], rk.at[f], band, f).wait_recv()
+        return c
+
+    lax.fori_loop(1, NF, got0, 0)
+    lane_s = lax.broadcasted_iota(jnp.int32, (STP, L), 1).astype(F32)
+
+    def ready(f, c):
+        row_p[1:2, 0:STICKS] = all_cols[f].astype(F32)
+        col = row_p[1:2, :]
+        kx = jnp.floor((col + 0.5) * (1.0 / N))
+        kx_of[f] = kx
+        ky = jnp.transpose(jnp.broadcast_to(col - N * kx, (L, STP)))
+        hot = jnp.where(lane_s == ky, 1.0, 0.0).astype(BF16)
+        along_y[f] = dot(hot, hr[0:L]).astype(BF16)
+        return c
+
+    lax.fori_loop(0, NF, ready, 0)
 
     def got1(d, c):
         b = lax.rem(band + d, NBAND)
@@ -213,7 +244,6 @@
     flipped = jnp.transpose(along)
     for f in range(NF):
         at_send[f] = flipped[f * ZP:(f + 1) * ZP]
-        at_send[f, ZP - 1:ZP, :] = cols_p[0:1, :]
 
     def go2(d, c):
         f = lax.rem(fft + d, NF)
@@ -223,110 +253,106 @@
     lax.fori_loop(1, NF, go2, 0)
     at_recv[0, fft] = at_send[fft]
 
-    srow = lax.broadcasted_iota(jnp.int32, (ZP, STP), 0)
-    kyrow = lax.broadcasted_iota(jnp.int32, (L, STP), 0).astype(F32)
-
-    def arrive(which, d, f):
-        if which == 0:
-            @pl.when(d > 0)
-            def _():
-                copy(at_send.at[f], at_recv.at[0, f], s2.at[0, f], r2.at[0, f],
-                     band, f).wait_recv()
-            copy(at_recv.at[0, f], at_recv.at[1, f], s2.at[1, f], r2.at[1, f],
-                 prv, fft).start()
-        else:
-            copy(at_recv.at[0, f], at_recv.at[1, f], s2.at[1, f], r2.at[1, f],
-                 prv, fft).wait_recv()
-
-    def orbital(which):
-        def spread(d, c):
-            f = lax.rem(fft + d, NF)
-            arrive(which, d, f)
-            blk = at_recv[which, f]
-            col = blk[ZP - 1:ZP, :]
-            kx = jnp.floor((col + 0.5) * (1.0 / N))
-            ky = col - N * kx
-            a = jnp.where(srow < ZL, blk, 0.0)
-            hot = jnp.where(kyrow == ky, 1.0, 0.0).astype(BF16)
-            a_hi = a.astype(BF16).astype(F32)
-            a_lo = a - a_hi
-            his, los = [], []
-            for x in range(ZL):
-                hit = kx == x
-                his.append(jnp.where(hit, a_hi, 0.0).astype(BF16))
-                los.append(jnp.where(hit, a_lo, 0.0).astype(BF16))
-            w = jnp.concatenate(his + los, axis=0)
-            g = lax.dot_general(w, hot, (((1,), (1,)), ((), ())),
-                                preferred_element_type=F32).astype(BF16)
-            g = jnp.concatenate([g[:BLK], g[BLK:]], axis=1)
-            tb[pl.ds(pl.multiple_of(f * BLK, 8), BLK), :] = fold(dot(g, hr[...]))
-            return c
-
-        lax.fori_loop(0, NF, spread, 0)
-        p = 1 - which
-        for z in range(ZL):
-            value = left_mul(lx[...], tb[pl.ds(z, L, stride=ZP), :])
-            phi[which, z] = value
-            rho = left_mul(lp[...], value * (value if p else phi[0, z]))
-            rho = right_mul(rho, hr[...])
-            send_f[p, :, z] = rho.reshape(NF, ZP, L)
-            if z % CHUNK == CHUNK - 1:
-                first = z - CHUNK + 1
-
-                def go(d, c):
-                    f = lax.rem(fft + d, NF)
-                    copy(send_f.at[p, f, first:first + CHUNK],
-                         recv_f3.at[p, pl.ds(fft * ZL + first, CHUNK)],
-                         sf.at[p, f], rf.at[p, fft], band, f).start()
-                    return c
-
-                lax.fori_loop(1, NF, go, 0)
+    def go2n(d, c):
+        f = lax.rem(fft + d, NF)
+        copy(at_send.at[f], at_recv.at[1, fft], s2.at[1, f], r2.at[1, fft], prv, f).start()
+        return c
+
+    lax.fori_loop(0, NF, go2n, 0)
+
+    def spread(which, f):
+        kx = kx_of[f]
+        a = at_recv[which, f]
+        a_hi = a.astype(BF16).astype(F32)
+        a_lo = a - a_hi
+        w = [jnp.where(kx == x, part, 0.0).astype(BF16)
+             for part in (a_hi, a_lo) for x in range(ZL)]
+        g = fold(dot(jnp.concatenate(w, axis=0), along_y[f]))
+        tb[f * BLK:(f + 1) * BLK, :] = g[:BLK] + g[BLK:]
+
+    def stick_block(which, d, b, f):
+        return copy(at_send.at[f], at_recv.at[which, f], s2.at[which, f], r2.at[which, f], b, f)
+
+    def own_arrives(d, c):
+        f = lax.rem(fft + d, NF)
+        stick_block(0, d, band, f).wait_recv()
+        return c
+
+    def next_arrives(f, c):
+        stick_block(1, f, nxt, f).wait_recv()
+        return c
+
+    def part(k, f):
+        step, first = k // PARTS, k % PARTS * CHUNK
+        p = step % 2
+        if step < 2:
+            return copy(send_f.at[p, f, first:first + CHUNK],
+                        recv_f3.at[p, pl.ds(fft * ZL + first, CHUNK)],
+                        sp.at[k, f], rf.at[p, fft], band, f)
+        return copy(send_b.at[p, f, first:first + CHUNK],
+                    recv_b.at[p, fft, first:first + CHUNK],
+                    sp.at[k, f], rb.at[p, fft], band, f)
+
+    def each_other(act):
+        lax.fori_loop(1, NF, lambda d, c: (act(lax.rem(fft + d, NF)), c)[1], 0)
+
+    def issue(k):
+        if k >= 2:
+            each_other(lambda f: part(k - 2, f).wait_send())
+        each_other(lambda f: part(k, f).start())
+
+    def forward(p, first, count):
+        for z in range(first, first + count):
+            rho = left_mul(lp[...], phi[0, z] * phi[1 - p, z])
+            send_f[p, :, z] = right_mul(rho, hr[...]).reshape(NF, ZP, L)
+
+    def orbital(which, first, count):
+        for z in range(first, first + count):
+            phi[which, z] = left_mul(lx[...], tb[pl.ds(z, L, stride=ZP), :])
+
+    def solve(p):
         recv_f3[p, pl.ds(fft * ZL, ZL)] = send_f[p, fft]
-
-    def solve(p, upto):
-        def got(d, c):
-            f = lax.rem(fft + d, NF)
-            copy(send_f.at[p, f], recv_f3.at[p, pl.ds(f * ZL, ZL)],
-                 sf.at[p, f], rf.at[p, f], band, f).wait_recv()
-            return c
-
-        lax.fori_loop(1, NF, got, 0)
+        each_other(lambda f: copy(
+            send_f.at[p, f], recv_f3.at[p, pl.ds(f * ZL, ZL)],
+            sp.at[0, f], rf.at[p, f], band, f).wait_recv())
         for x in range(ZL):
             data = recv_f[p, pl.ds(x, L, stride=ZP), :]
             spec = left_mul(lx[...], data) * coul[x]
             send_b[p, :, x] = left_mul(lp[...], spec).reshape(NF, ZP, L)
-            if x % CHUNK == CHUNK - 1 and x < upto:
-                give(p, x - CHUNK + 1)
-
-    def give(p, first):
-        def go(d, c):
-            f = lax.rem(fft + d, NF)
-            copy(send_b.at[p, f, first:first + CHUNK],
-                 recv_b.at[p, fft, first:first + CHUNK],
-                 sb.at[p, f], rb.at[p, fft], band, f).start()
-            return c
-
-        lax.fori_loop(1, NF, go, 0)
 
     def backward(p):
         def got(d, c):
             f = lax.rem(fft + d, NF)
-            copy(send_b.at[p, f], recv_b.at[p, f], sb.at[p, f], rb.at[p, f],
+            copy(send_b.at[p, f], recv_b.at[p, f], sp.at[0, f], rb.at[p, f],
                  band, f).wait_recv()
-            tb2[pl.ds(pl.multiple_of(f * BLK, 8), BLK), :] = right_mul(
-                recv_b[p, f].reshape(BLK, L), hr[...])
             return c
 
-        tb2[pl.ds(pl.multiple_of(fft * BLK, 8), BLK), :] = right_mul(
-            send_b[p, fft].reshape(BLK, L), hr[...])
+        recv_b[p, fft] = send_b[p, fft]
         lax.fori_loop(1, NF, got, 0)
-
-    orbital(0)
-    orbital(1)
-    solve(1, EARLY)
-    solve(0, ZL)
-    for first in range(EARLY, ZL, CHUNK):
-        give(1, first)
+        for f in range(NF):
+            tb2[f * BLK:(f + 1) * BLK, :] = right_mul(recv_b[p, f].reshape(BLK, L), hr[...])
+
+    lax.fori_loop(1, NF, own_arrives, 0)
+    for f in range(NF):
+        spread(0, f)
+    orbital(0, 0, ZL)
+    lax.fori_loop(0, NF, next_arrives, 0)
+    for f in range(NF):
+        spread(1, f)
+    for n in range(PARTS):
+        orbital(1, n * CHUNK, CHUNK)
+        forward(0, n * CHUNK, CHUNK)
+        if n < 2:
+            issue(n)
+    forward(1, 0, ZL)
+    for k in range(2, 5):
+        issue(k)
+    solve(0)
+    for k in range(5, 8):
+        issue(k)
+    solve(1)
+    for k in range(8, 11):
+        issue(k)
     backward(0)
     far = lax.rem(band, 16) == 15
     nxt_row = (nxt // 16) * 16
@@ -361,6 +387,7 @@
             acc[z] = (v * phi[1, z])[:N]
             send_v[z] = (v * phi[0, z])[:N]
         send_term(first, count, hop)
+    issue(11)
     for first, count, hop in ROUTES:
         if hop:
             @pl.when(lax.rem(band, 16) == 2 * hop)
@@ -398,19 +425,16 @@
 
     def left2(d, c):
         f = lax.rem(fft + d, NF)
-        copy(at_send.at[f], at_recv.at[0, f], s2.at[0, f], r2.at[0, f], band, f).wait_send()
-        for p in range(2):
-            copy(send_f.at[p, f], recv_f3.at[p, pl.ds(f * ZL, ZL)], sf.at[p, f], rf.at[p, f],
-                 band, f).wait_send()
-            copy(send_b.at[p, f], recv_b.at[p, f], sb.at[p, f], rb.at[p, f],
-                 band, f).wait_send()
+        copy(cols, all_cols.at[f], sk.at[f], rk.at[f], band, f).wait_send()
+        stick_block(0, d, band, f).wait_send()
+        for k in (10, 11):
+            part(k, f).wait_send()
         return c
 
     lax.fori_loop(1, NF, left2, 0)
 
     def left2n(f, c):
-        copy(at_recv.at[0, f], at_recv.at[1, f], s2.at[1, f], r2.at[1, f],
-             prv, fft).wait_send()
+        stick_block(1, f, prv, f).wait_send()
         return c
 
     lax.fori_loop(0, NF, left2n, 0)
@@ -446,6 +470,9 @@
             pltpu.VMEM((STICKS, L), F32),
             pltpu.VMEM((1, NBAND * CAPP), jnp.int32),
             pltpu.VMEM((8, STP), F32),
+            pltpu.VMEM((NF, 1, STICKS), jnp.int32),
+            pltpu.VMEM((NF, 1, STP), F32),
+            pltpu.VMEM((NF, STP, 2 * L), BF16),
             pltpu.VMEM((NF, ZP, STP), F32),
             pltpu.VMEM((2, NF, ZP, STP), F32),
             pltpu.VMEM((2, ZL, L, L), F32),
@@ -460,16 +487,17 @@
             pltpu.VMEM((ZL, N, L), F32),
             pltpu.VMEM((ZL, N, L), F32),
             pltpu.VMEM((4, N, L), F32),
+            dma((NF,)), dma((NF,)),
             dma((NBAND,)), dma((NBAND,)),
             dma((2, NF)), dma((2, NF)),
-            dma((2, NF)), dma((2, NF)),
-            dma((2, NF)), dma((2, NF)),
+            dma((4 * PARTS, NF)), dma((2, NF)), dma((2, NF)),
             dma, dma, dma, dma,
             dma((6,)),
         ],
         compiler_params=pltpu.CompilerParams(
-            collective_id=0, has_side_effects=True, vmem_limit_bytes=60 * 1024 * 1024),
-    )(coefficients, owned_sticks, stick_counts, stick_columns, band_order, tables)
+            collective_id=0, has_side_effects=True, vmem_limit_bytes=48 * 1024 * 1024),
+    )(*[pltpu.with_memory_space_constraint(a, pltpu.HBM) for a in (
+        coefficients, owned_sticks, stick_counts, stick_columns, band_order, tables)])
     return out.reshape(1, ZL, N * N)
 
 

time: 91 us -> 87.6 us (0.963)
  Pallas kernels: 88.4 us -> 86.6 us
  local copies, waits for them, and re-layouts: 2.13 us -> 0.91 us
    pallas_call x1, Pallas kernels: 88.4 us -> 86.6 us  [local(): pl.pallas_call(kernel, out_shape=jax.ShapeDtypeStruct((ZL, 1, N * N), F32...]
    unnamed x1, local copies, waits for them, and re-layouts: 2.13 us -> 0.91 us
where the time goes in v3:
time: 87.6 us
  Pallas kernels  86.6 us (99%)
  local copies, waits for them, and re-layouts  0.91 us (1%)
    pallas_call x1, Pallas kernels, local(): pl.pallas_call(kernel, out_shape=jax.ShapeDtypeStruct((ZL, 1, N * N), F32...  86.6 us

profile of v3, /device:TPU:2, one launch (start us, length us, event | category | flops | bytes accessed | tf_op | source)
XLA Modules:
  0.0 87.6 jit_solution(15288766985318586798)
XLA Ops:
  0.0 86.6 %shard_map.64 = f32[15,1,14400]{2,1,0:T(1,128)S(1)} custom-call(f32[32,2640]{1,0:T(8,128)} %coef_h.1, s32[1,704]{1,0:T(1,128)} %owned_h.1, s32[1,352]{1,0:T(1,128)} %counts_h.1, s32[1,352]{1,0:T(1,128)} %cols_h.1, s32[32]{0:T(128)} %order_h.1, bf16[768,256]{1,0:T(8,128)(2,1)} %constant.2.clone.tables_h), custom_call_target="tpu_custom_call" | custom-call | tf_op jit(solution)/shard_map/pallas_call | solution.py:453
  86.6 0.9 %copy.8 = f32[1,15,14400]{2,0,1:T(1,128)} copy(f32[1,15,14400]{2,0,1:T(1,128)S(1)} %bitcast.1) | data formatting | bytes 1728000

commit v4 on v3

--- a/solution.py
+++ b/solution.py
@@ -60,6 +60,7 @@
         right(place(k, zpad)),
         left(plain),
         left(place(zpad, k)),
+        left(place(k, zpad)),
     ], axis=0)
 
 
@@ -90,13 +91,14 @@
     coef_h, owned_h, counts_h, cols_h, order_h, tables_h, out,
     coef, owned, counts, cols, order, tables,
     stage, stage3, send1, recv1, sel, keep, owned_p, row_p, all_cols, kx_of, along_y, at_send, at_recv, phi, tb, tb2,
-    coul, send_f, recv_f3, send_b, recv_b, send_v, recv_v, acc, relay,
+    coul, send_f, recv_f, send_b, recv_b, send_v, recv_v, acc, relay,
     sk, rk, s1, r1, s2, r2, sp, rf, rb, sv, rv, rr, sr, sin,
 ):
     hr = tables.at[0:2 * L]
     hrz = tables.at[2 * L:4 * L]
     lx = tables.at[4 * L:5 * L]
     lp = tables.at[5 * L:6 * L]
+    lz = tables.at[6 * L:7 * L]
     band = lax.axis_index("band")
     fft = lax.axis_index("fft")
     nxt = lax.rem(band + 1, NBAND)
@@ -107,8 +109,6 @@
             src_ref=src, dst_ref=dst, send_sem=ssem, recv_sem=rsem,
             device_id=(b, f), device_id_type=pl.DeviceIdType.MESH,
         )
-
-    recv_f = recv_f3.reshape(2, L * ZP, L)
 
     barrier = pltpu.get_barrier_semaphore()
 
@@ -176,8 +176,6 @@
 
     tb[...] = jnp.zeros(tb.shape, F32)
     tb2[N * ZP:, :] = jnp.zeros(((L - N) * ZP, L), F32)
-    for p in range(2):
-        recv_f[p, N * ZP:, :] = jnp.zeros(((L - N) * ZP, L), F32)
     for n in (2, 3, 5):
         loads[n].wait()
     owned_p[...] = jnp.full(owned_p.shape, -1, jnp.int32)
@@ -283,15 +281,11 @@
         return c
 
     def part(k, f):
-        step, first = k // PARTS, k % PARTS * CHUNK
-        p = step % 2
-        if step < 2:
-            return copy(send_f.at[p, f, first:first + CHUNK],
-                        recv_f3.at[p, pl.ds(fft * ZL + first, CHUNK)],
-                        sp.at[k, f], rf.at[p, fft], band, f)
-        return copy(send_b.at[p, f, first:first + CHUNK],
-                    recv_b.at[p, fft, first:first + CHUNK],
-                    sp.at[k, f], rb.at[p, fft], band, f)
+        step, n = k // PARTS, k % PARTS
+        p, first = step // 2, n * CHUNK
+        src, dst, rsem = (send_b, recv_b, rb) if step % 2 else (send_f, recv_f, rf)
+        return copy(src.at[p, f, first:first + CHUNK], dst.at[p, fft, first:first + CHUNK],
+                    sp.at[k, f], rsem.at[p * PARTS + n, fft], band, f)
 
     def each_other(act):
         lax.fori_loop(1, NF, lambda d, c: (act(lax.rem(fft + d, NF)), c)[1], 0)
@@ -301,36 +295,42 @@
             each_other(lambda f: part(k - 2, f).wait_send())
         each_other(lambda f: part(k, f).start())
 
-    def forward(p, first, count):
-        for z in range(first, first + count):
-            rho = left_mul(lp[...], phi[0, z] * phi[1 - p, z])
-            send_f[p, :, z] = right_mul(rho, hr[...]).reshape(NF, ZP, L)
+    def arrived_parts(dst, rsem, p, n):
+        first = n * CHUNK
+        each_other(lambda f: copy(
+            dst.at[p, f, first:first + CHUNK], dst.at[p, f, first:first + CHUNK],
+            sp.at[0, f], rsem.at[p * PARTS + n, f], band, f).wait_recv())
+
+    def density(p):
+        for z in range(ZL):
+            tb[pl.ds(z, L, stride=ZP), :] = left_mul(lx[...], phi[0, z] * phi[1 - p, z])
+
+    def forward(p, n):
+        first = n * CHUNK
+        for f in range(NF):
+            rows = f * BLK + first * ZP
+            send_f[p, f, first:first + CHUNK] = right_mul(
+                tb[rows:rows + CHUNK * ZP, :], hr[...]).reshape(CHUNK, ZP, L)
+        recv_f[p, fft, first:first + CHUNK] = send_f[p, fft, first:first + CHUNK]
 
     def orbital(which, first, count):
         for z in range(first, first + count):
             phi[which, z] = left_mul(lx[...], tb[pl.ds(z, L, stride=ZP), :])
 
-    def solve(p):
-        recv_f3[p, pl.ds(fft * ZL, ZL)] = send_f[p, fft]
-        each_other(lambda f: copy(
-            send_f.at[p, f], recv_f3.at[p, pl.ds(f * ZL, ZL)],
-            sp.at[0, f], rf.at[p, f], band, f).wait_recv())
-        for x in range(ZL):
-            data = recv_f[p, pl.ds(x, L, stride=ZP), :]
-            spec = left_mul(lx[...], data) * coul[x]
+    def solve(p, n):
+        arrived_parts(recv_f, rf, p, n)
+        for x in range(n * CHUNK, (n + 1) * CHUNK):
+            spec = left_mul(lz[...], recv_f[p, :, x].reshape(L, L)) * coul[x]
             send_b[p, :, x] = left_mul(lp[...], spec).reshape(NF, ZP, L)
 
     def backward(p):
-        def got(d, c):
-            f = lax.rem(fft + d, NF)
-            copy(send_b.at[p, f], recv_b.at[p, f], sp.at[0, f], rb.at[p, f],
-                 band, f).wait_recv()
-            return c
-
         recv_b[p, fft] = send_b[p, fft]
-        lax.fori_loop(1, NF, got, 0)
-        for f in range(NF):
-            tb2[f * BLK:(f + 1) * BLK, :] = right_mul(recv_b[p, f].reshape(BLK, L), hr[...])
+        for n in range(PARTS):
+            arrived_parts(recv_b, rb, p, n)
+            for f in range(NF):
+                rows = f * BLK + n * CHUNK * ZP
+                tb2[rows:rows + CHUNK * ZP, :] = right_mul(
+                    recv_b[p, f, n * CHUNK:(n + 1) * CHUNK].reshape(CHUNK * ZP, L), hr[...])
 
     lax.fori_loop(1, NF, own_arrives, 0)
     for f in range(NF):
@@ -339,20 +339,21 @@
     lax.fori_loop(0, NF, next_arrives, 0)
     for f in range(NF):
         spread(1, f)
+    orbital(1, 0, ZL)
+    density(0)
     for n in range(PARTS):
-        orbital(1, n * CHUNK, CHUNK)
-        forward(0, n * CHUNK, CHUNK)
+        forward(0, n)
         if n < 2:
             issue(n)
-    forward(1, 0, ZL)
-    for k in range(2, 5):
-        issue(k)
-    solve(0)
-    for k in range(5, 8):
-        issue(k)
-    solve(1)
-    for k in range(8, 11):
-        issue(k)
+    density(1)
+    for n in range(PARTS):
+        forward(1, n)
+    issue(2)
+    for n in range(PARTS):
+        solve(0, n)
+        issue(3 + n)
+    issue(6)
+    issue(7)
     backward(0)
     far = lax.rem(band, 16) == 15
     nxt_row = (nxt // 16) * 16
@@ -387,7 +388,10 @@
             acc[z] = (v * phi[1, z])[:N]
             send_v[z] = (v * phi[0, z])[:N]
         send_term(first, count, hop)
-    issue(11)
+    issue(8)
+    for n in range(PARTS):
+        solve(1, n)
+        issue(9 + n)
     for first, count, hop in ROUTES:
         if hop:
             @pl.when(lax.rem(band, 16) == 2 * hop)
@@ -461,7 +465,7 @@
             pltpu.VMEM((1, STICKS), jnp.int32),
             pltpu.VMEM((1, STICKS), jnp.int32),
             pltpu.SMEM((NBAND,), jnp.int32),
-            pltpu.VMEM((6 * L, 2 * L), BF16),
+            pltpu.VMEM((7 * L, 2 * L), BF16),
             pltpu.VMEM((NBAND * CAPP, L), F32),
             pltpu.VMEM((NBAND, CAPP, L), F32),
             pltpu.VMEM((NBAND, CAPP, L), F32),
@@ -480,7 +484,7 @@
             pltpu.VMEM((L * ZP, L), F32),
             pltpu.VMEM((ZL, L, L), F32),
             pltpu.VMEM((2, NF, ZL, ZP, L), F32),
-            pltpu.VMEM((2, L, ZP, L), F32),
+            pltpu.VMEM((2, NF, ZL, ZP, L), F32),
             pltpu.VMEM((2, NF, ZL, ZP, L), F32),
             pltpu.VMEM((2, NF, ZL, ZP, L), F32),
             pltpu.VMEM((ZL, N, L), F32),
@@ -490,7 +494,7 @@
             dma((NF,)), dma((NF,)),
             dma((NBAND,)), dma((NBAND,)),
             dma((2, NF)), dma((2, NF)),
-            dma((4 * PARTS, NF)), dma((2, NF)), dma((2, NF)),
+            dma((4 * PARTS, NF)), dma((2 * PARTS, NF)), dma((2 * PARTS, NF)),
             dma, dma, dma, dma,
             dma((6,)),
         ],

time: 87.6 us -> 84.8 us (0.968)
  Pallas kernels: 86.6 us -> 83.8 us
    pallas_call x1, Pallas kernels: 86.6 us -> 83.8 us  [local(): pl.pallas_call(kernel, out_shape=jax.ShapeDtypeStruct((ZL, 1, N * N), F32...]
where the time goes in v4:
time: 84.8 us
  Pallas kernels  83.8 us (99%)
  local copies, waits for them, and re-layouts  0.91 us (1%)
    pallas_call x1, Pallas kernels, local(): pl.pallas_call(kernel, out_shape=jax.ShapeDtypeStruct((ZL, 1, N * N), F32...  83.8 us

profile of v4, /device:TPU:2, one launch (start us, length us, event | category | flops | bytes accessed | tf_op | source)
XLA Modules:
  0.0 84.8 jit_solution(13340494624995474960)
XLA Ops:
  0.0 83.8 %shard_map.64 = f32[15,1,14400]{2,1,0:T(1,128)S(1)} custom-call(f32[32,2640]{1,0:T(8,128)} %coef_h.1, s32[1,704]{1,0:T(1,128)} %owned_h.1, s32[1,352]{1,0:T(1,128)} %counts_h.1, s32[1,352]{1,0:T(1,128)} %cols_h.1, s32[32]{0:T(128)} %order_h.1, bf16[896,256]{1,0:T(8,128)(2,1)} %constant.2.clone.tables_h), custom_call_target="tpu_custom_call" | custom-call | tf_op jit(solution)/shard_map/pallas_call | solution.py:457
  83.8 0.9 %copy.8 = f32[1,15,14400]{2,0,1:T(1,128)} copy(f32[1,15,14400]{2,0,1:T(1,128)S(1)} %bitcast.1) | data formatting | bytes 1728000

commit v5 on v4

--- a/solution.py
+++ b/solution.py
@@ -22,7 +22,14 @@
 BLK = ZL * ZP
 CHUNK = 5
 PARTS = ZL // CHUNK
-ROUTES = ((0, 4, 6), (4, 4, 1), (8, 4, 7), (12, 3, 0))
+SEQUENCE = (
+    [(1, 0, 0)]
+    + [(0, 0, n) for n in range(PARTS)]
+    + [(0, 1, n) for n in range(PARTS)]
+    + [(1, 0, n) for n in range(1, PARTS)]
+    + [(1, 1, n) for n in range(PARTS)]
+)
+ROUTES = ((0, 3, 6), (3, 3, 1), (6, 3, 5), (9, 2, 2), (11, 2, 7), (13, 2, 0))
 COULOMB = 0.25
 EXCHANGE_FRACTION = 0.25
 F32 = jnp.float32
@@ -110,33 +117,36 @@
             device_id=(b, f), device_id_type=pl.DeviceIdType.MESH,
         )
 
-    barrier = pltpu.get_barrier_semaphore()
-
-    def hello_band(d, c):
-        pl.semaphore_signal(
-            barrier, inc=1, device_id=(lax.rem(band + d, NBAND), fft),
-            device_id_type=pl.DeviceIdType.MESH)
-        return c
-
-    lax.fori_loop(1, NBAND, hello_band, 0)
-
-    def hello_fft(d, c):
-        f = lax.rem(fft + d, NF)
-        pl.semaphore_signal(
-            barrier, inc=1, device_id=(band, f), device_id_type=pl.DeviceIdType.MESH)
-        pl.semaphore_signal(
-            barrier, inc=1, device_id=(nxt, f), device_id_type=pl.DeviceIdType.MESH)
-        return c
-
-    lax.fori_loop(1, NF, hello_fft, 0)
-
     loads = [
         pltpu.make_async_copy(src, dst, sin.at[n])
         for n, (src, dst) in enumerate([
             (coef_h, coef), (order_h, order), (owned_h, owned), (counts_h, counts),
             (cols_h, cols), (tables_h, tables)])
     ]
-    for load in loads:
+    loads[0].start()
+    loads[1].start()
+
+    barrier = pltpu.get_barrier_semaphore()
+
+    def hello_band(d, c):
+        pl.semaphore_signal(
+            barrier, inc=1, device_id=(lax.rem(band + d, NBAND), fft),
+            device_id_type=pl.DeviceIdType.MESH)
+        return c
+
+    lax.fori_loop(1, NBAND, hello_band, 0)
+
+    def hello_fft(d, c):
+        f = lax.rem(fft + d, NF)
+        pl.semaphore_signal(
+            barrier, inc=1, device_id=(band, f), device_id_type=pl.DeviceIdType.MESH)
+        pl.semaphore_signal(
+            barrier, inc=1, device_id=(nxt, f), device_id_type=pl.DeviceIdType.MESH)
+        return c
+
+    lax.fori_loop(1, NF, hello_fft, 0)
+
+    for load in loads[2:]:
         load.start()
 
     stage[...] = jnp.zeros(stage.shape, F32)
@@ -149,7 +159,7 @@
     loads[1].wait()
 
     def reorder(j, c):
-        send1[j] = stage3[order[j]]
+        send1[j] = stage3[order[j]][:CAP]
         return c
 
     lax.fori_loop(0, NBAND, reorder, 0)
@@ -166,15 +176,14 @@
 
     lax.fori_loop(1, NF, go0, 0)
 
-    def go1(d, c):
+    for d in sorted(range(1, NBAND), key=lambda d: (abs(d % 16 - 8), d)):
         b = lax.rem(band + d, NBAND)
         copy(send1.at[b], recv1.at[band], s1.at[b], r1.at[band], b, fft).start()
-        return c
-
-    lax.fori_loop(1, NBAND, go1, 0)
     recv1[band] = send1[band]
 
     tb[...] = jnp.zeros(tb.shape, F32)
+    recv_f[...] = jnp.zeros(recv_f.shape, F32)
+    recv_b[...] = jnp.zeros(recv_b.shape, F32)
     tb2[N * ZP:, :] = jnp.zeros(((L - N) * ZP, L), F32)
     for n in (2, 3, 5):
         loads[n].wait()
@@ -232,7 +241,8 @@
 
     lax.fori_loop(1, NBAND, got1, 0)
 
-    arrived = halves(recv1[...].reshape(NBAND * CAPP, L))
+    stage3[:, 0:CAP, :] = recv1[...]
+    arrived = halves(stage3[...].reshape(NBAND * CAPP, L))
     picked = dot(sel[...], arrived)
     kept = keep[...] > 0.0
     hi = jnp.where(kept, picked[:, :L], 0.0).astype(BF16)
@@ -281,10 +291,11 @@
         return c
 
     def part(k, f):
-        step, n = k // PARTS, k % PARTS
-        p, first = step // 2, n * CHUNK
-        src, dst, rsem = (send_b, recv_b, rb) if step % 2 else (send_f, recv_f, rf)
-        return copy(src.at[p, f, first:first + CHUNK], dst.at[p, fft, first:first + CHUNK],
+        p, back, n = SEQUENCE[k]
+        first = n * CHUNK
+        src, dst, rsem = (send_b, recv_b, rb) if back else (send_f, recv_f, rf)
+        return copy(src.at[p, f, first:first + CHUNK, 0:ZL],
+                    dst.at[p, fft, first:first + CHUNK, 0:ZL],
                     sp.at[k, f], rsem.at[p * PARTS + n, fft], band, f)
 
     def each_other(act):
@@ -298,7 +309,8 @@
     def arrived_parts(dst, rsem, p, n):
         first = n * CHUNK
         each_other(lambda f: copy(
-            dst.at[p, f, first:first + CHUNK], dst.at[p, f, first:first + CHUNK],
+            dst.at[p, f, first:first + CHUNK, 0:ZL],
+            dst.at[p, f, first:first + CHUNK, 0:ZL],
             sp.at[0, f], rsem.at[p * PARTS + n, f], band, f).wait_recv())
 
     def density(p):
@@ -336,6 +348,11 @@
     for f in range(NF):
         spread(0, f)
     orbital(0, 0, ZL)
+    density(1)
+    forward(1, 0)
+    issue(0)
+    for n in range(1, PARTS):
+        forward(1, n)
     lax.fori_loop(0, NF, next_arrives, 0)
     for f in range(NF):
         spread(1, f)
@@ -343,17 +360,12 @@
     density(0)
     for n in range(PARTS):
         forward(0, n)
-        if n < 2:
-            issue(n)
-    density(1)
-    for n in range(PARTS):
-        forward(1, n)
-    issue(2)
+        issue(1 + n)
     for n in range(PARTS):
         solve(0, n)
-        issue(3 + n)
-    issue(6)
-    issue(7)
+        issue(1 + PARTS + n)
+    for n in range(1, PARTS):
+        issue(2 * PARTS + n)
     backward(0)
     far = lax.rem(band, 16) == 15
     nxt_row = (nxt // 16) * 16
@@ -388,10 +400,9 @@
             acc[z] = (v * phi[1, z])[:N]
             send_v[z] = (v * phi[0, z])[:N]
         send_term(first, count, hop)
-    issue(8)
     for n in range(PARTS):
         solve(1, n)
-        issue(9 + n)
+        issue(3 * PARTS + n)
     for first, count, hop in ROUTES:
         if hop:
             @pl.when(lax.rem(band, 16) == 2 * hop)
@@ -431,7 +442,7 @@
         f = lax.rem(fft + d, NF)
         copy(cols, all_cols.at[f], sk.at[f], rk.at[f], band, f).wait_send()
         stick_block(0, d, band, f).wait_send()
-        for k in (10, 11):
+        for k in (4 * PARTS - 2, 4 * PARTS - 1):
             part(k, f).wait_send()
         return c
 
@@ -468,8 +479,8 @@
             pltpu.VMEM((7 * L, 2 * L), BF16),
             pltpu.VMEM((NBAND * CAPP, L), F32),
             pltpu.VMEM((NBAND, CAPP, L), F32),
-            pltpu.VMEM((NBAND, CAPP, L), F32),
-            pltpu.VMEM((NBAND, CAPP, L), F32),
+            pltpu.VMEM((NBAND, CAP, L), F32),
+            pltpu.VMEM((NBAND, CAP, L), F32),
             pltpu.VMEM((STICKS, NBAND * CAPP), BF16),
             pltpu.VMEM((STICKS, L), F32),
             pltpu.VMEM((1, NBAND * CAPP), jnp.int32),

time: 84.8 us -> 78.9 us (0.930)
  Pallas kernels: 83.8 us -> 77.8 us
    pallas_call x1, Pallas kernels: 83.8 us -> 77.8 us  [local(): pl.pallas_call(kernel, out_shape=jax.ShapeDtypeStruct((ZL, 1, N * N), F32...]
where the time goes in v5:
time: 78.9 us; the launch traced here: 78.7 us
  Pallas kernels  77.8 us (99%)
  local copies, waits for them, and re-layouts  0.91 us (1%)
    pallas_call x1, Pallas kernels, local(): pl.pallas_call(kernel, out_shape=jax.ShapeDtypeStruct((ZL, 1, N * N), F32...  77.8 us

profile of v5, /device:TPU:2, one launch (start us, length us, event | category | flops | bytes accessed | tf_op | source)
XLA Modules:
  0.0 78.7 jit_solution(7327806711569009215)
XLA Ops:
  0.0 77.8 %shard_map.64 = f32[15,1,14400]{2,1,0:T(1,128)S(1)} custom-call(f32[32,2640]{1,0:T(8,128)} %coef_h.1, s32[1,704]{1,0:T(1,128)} %owned_h.1, s32[1,352]{1,0:T(1,128)} %counts_h.1, s32[1,352]{1,0:T(1,128)} %cols_h.1, s32[32]{0:T(128)} %order_h.1, bf16[896,256]{1,0:T(8,128)(2,1)} %constant.2.clone.tables_h), custom_call_target="tpu_custom_call" | custom-call | tf_op jit(solution)/shard_map/pallas_call | solution.py:468
  77.8 0.9 %copy.8 = f32[1,15,14400]{2,0,1:T(1,128)} copy(f32[1,15,14400]{2,0,1:T(1,128)S(1)} %bitcast.1) | data formatting | bytes 1728000

commit v6 on v5

--- a/solution.py
+++ b/solution.py
@@ -302,8 +302,8 @@
         lax.fori_loop(1, NF, lambda d, c: (act(lax.rem(fft + d, NF)), c)[1], 0)
 
     def issue(k):
-        if k >= 2:
-            each_other(lambda f: part(k - 2, f).wait_send())
+        if k >= 3:
+            each_other(lambda f: part(k - 3, f).wait_send())
         each_other(lambda f: part(k, f).start())
 
     def arrived_parts(dst, rsem, p, n):
@@ -411,12 +411,10 @@
                 from_relay(first, count).start()
 
     backward(1)
+    to_next(0, ZL).wait_recv()
     for z in range(ZL):
         v = left_mul(lx[...], tb2[pl.ds(z, L, stride=ZP), :])
-        acc[z] += (v * phi[0, z])[:N]
-    to_next(0, ZL).wait_recv()
-    for z in range(ZL):
-        tb[pl.ds(z, N, stride=ZP), :] = acc[z] + recv_v[z]
+        tb[pl.ds(z, N, stride=ZP), :] = (v * phi[0, z])[:N] + acc[z] + recv_v[z]
 
     lane = lax.broadcasted_iota(jnp.int32, (ZP, L), 1)
     total = N * N
@@ -442,7 +440,7 @@
         f = lax.rem(fft + d, NF)
         copy(cols, all_cols.at[f], sk.at[f], rk.at[f], band, f).wait_send()
         stick_block(0, d, band, f).wait_send()
-        for k in (4 * PARTS - 2, 4 * PARTS - 1):
+        for k in range(4 * PARTS - 3, 4 * PARTS):
             part(k, f).wait_send()
         return c
 

time: 78.9 us -> 78.8 us (level)
  no operation moved by 1% of the time
where the time goes in v6:
time: 78.8 us; the launch traced here: 78.7 us
  Pallas kernels  77.8 us (99%)
  local copies, waits for them, and re-layouts  0.91 us (1%)
    pallas_call x1, Pallas kernels, local(): pl.pallas_call(kernel, out_shape=jax.ShapeDtypeStruct((ZL, 1, N * N), F32...  77.8 us

profile of v6, /device:TPU:2, one launch (start us, length us, event | category | flops | bytes accessed | tf_op | source)
XLA Modules:
  0.0 78.7 jit_solution(15718762724745605771)
XLA Ops:
  0.0 77.8 %shard_map.64 = f32[15,1,14400]{2,1,0:T(1,128)S(1)} custom-call(f32[32,2640]{1,0:T(8,128)} %coef_h.1, s32[1,704]{1,0:T(1,128)} %owned_h.1, s32[1,352]{1,0:T(1,128)} %counts_h.1, s32[1,352]{1,0:T(1,128)} %cols_h.1, s32[32]{0:T(128)} %order_h.1, bf16[896,256]{1,0:T(8,128)(2,1)} %constant.2.clone.tables_h), custom_call_target="tpu_custom_call" | custom-call | tf_op jit(solution)/shard_map/pallas_call | solution.py:466
  77.8 0.9 %copy.8 = f32[1,15,14400]{2,0,1:T(1,128)} copy(f32[1,15,14400]{2,0,1:T(1,128)S(1)} %bitcast.1) | data formatting | bytes 1728000
